TPU v7x, 32 devices: a whole 2x2x4 slice. The times are simulated.
32 devices in a mesh: groups: 2 (over x), col: 16 (over z, y, core).
Axes of the slice: x: 2, y: 2, z: 4, core: 2. Of those that a mesh axis runs over, the one named last changes fastest.
Arguments:
- features: bfloat16 [32, 8, 8192], P(('groups', 'col')), parts along dimension 0
- zone_ids: int32 [32], P(('groups', 'col')), parts along dimension 0, may hold values from 0 to 7, as said below
- golden_owner: int32 [16], P('groups'), parts along dimension 0, may hold values from 0 to 15, as said below
- defect_mask: int32 [32, 8, 128], P(('groups', 'col')), parts along dimension 0, may hold values 0 or 1
- kernels: bfloat16 [2, 576, 64], replicated, may hold values from -0.25 to 0.25
Outputs:
- score: float32 [32, 8, 128], P(('groups', 'col')), parts along dimension 0
There are 2 independent parts, one for each index of `groups`. A program takes and returns all parts, laid end to end along the dimension named above; an argument that names none is the same for every part. Nothing has to cross between parts.
Inputs may be any that keep to these rules, and one draw needn't show every extreme that they name: `zone_ids`: every zone holds at least one die. golden_owner[z] is a die of zone z.
All inputs are finite; a program needn't handle non-finite values. No bound on the sum of `defect_mask` on one device may be relied on, other than what follows from the above.
Results may differ from a plain program's by a relative error of at most 0.0039.
Values may be sent and summed in bfloat16 or wider, within the bound.
No kernel may reach another device: no remote copies, remote signals or barrier semaphores. Data moves between devices by JAX's collectives and lax.ppermute only.
A program may use at most 64 MiB of HBM per device.

v0:
```python
import jax
import jax.numpy as jnp
from jax import lax
from jax.sharding import PartitionSpec as P

C = 64
SHIFT = 6
BOX = 5
Z = 8


def box_sum(plane):
    rows = plane.shape[0]
    cols = plane.shape[1]
    reach = BOX // 2
    padded = jnp.pad(plane, ((reach, reach), (reach, reach)))
    across = padded[0:rows]
    for offset in range(1, BOX):
        across = across + padded[offset : offset + rows]
    total = across[:, 0:cols]
    for offset in range(1, BOX):
        total = total + across[:, offset : offset + cols]
    return total


def channel_sum(values, chans):
    return jnp.sum(values.reshape(values.shape[0], -1, chans), axis=-1)


def align_golden(test_tile, golden_tile, chans):
    height, spread = test_tile.shape
    width = spread // chans
    side = 2 * SHIFT + 1
    test_f = test_tile.astype(jnp.float32)
    padded = jnp.pad(golden_tile, ((SHIFT, SHIFT), (SHIFT * chans, SHIFT * chans)))
    padded_f = padded.astype(jnp.float32)
    golden_sq = channel_sum(padded_f * padded_f, chans)
    self_energy = box_sum(channel_sum(test_f * test_f, chans))

    def row_step(carry, row_off):
        numer, denom = carry
        band = lax.dynamic_slice_in_dim(padded, row_off, height, 0).astype(jnp.float32)
        sq_band = lax.dynamic_slice_in_dim(golden_sq, row_off, height, 0)
        for col_off in range(side):
            moved = band[:, col_off * chans : col_off * chans + spread]
            cross = box_sum(channel_sum(test_f * moved, chans))
            other = box_sum(sq_band[:, col_off : col_off + width])
            expo = jnp.exp(32.0 * cross / jnp.sqrt(self_energy * other + 1e-05))
            numer = numer + jnp.repeat(expo, chans, axis=1) * moved
            denom = denom + expo
        return ((numer, denom), None)

    start = (jnp.zeros((height, spread), jnp.float32), jnp.zeros((height, width), jnp.float32))
    (numer, denom), _ = lax.scan(row_step, start, jnp.arange(side, dtype=jnp.int32))
    return numer / jnp.repeat(denom, chans, axis=1)


def conv_three(tile, kernel):
    height, width, chans = tile.shape
    padded = jnp.pad(tile, ((1, 1), (1, 1), (0, 0)))
    windows = []
    for tap in range(9):
        row_off = tap // 3
        col_off = tap % 3
        windows.append(
            padded[row_off : row_off + height, col_off : col_off + width].reshape(
                height * width, chans
            )
        )
    stacked = jnp.concatenate(windows, axis=1)
    total = jnp.dot(stacked, kernel, preferred_element_type=jnp.float32)
    return total.reshape(height, width, kernel.shape[1])


def body(features, zone_ids, golden_owner, defect_mask, kernels):
    height = features.shape[1]
    width = defect_mask.shape[2]
    my_zone = zone_ids[0]
    wanted = golden_owner[my_zone]
    piece = lax.all_gather(features, "col", axis=0, tiled=True)
    positions = jnp.arange(piece.shape[0], dtype=jnp.int32)
    chosen = jnp.where((positions == wanted)[:, None, None], piece, jnp.zeros_like(piece))
    golden = jnp.sum(chosen, axis=0, keepdims=True)
    test_tile = features[0]
    aligned = align_golden(test_tile, golden[0], C)
    residual = (
        (test_tile.astype(jnp.float32) - aligned).astype(jnp.bfloat16).reshape(height, width, C)
    )
    hidden = jax.nn.relu(conv_three(residual, kernels[0])).astype(jnp.bfloat16)
    refined = residual.astype(jnp.float32) + conv_three(hidden, kernels[1])
    energy = jnp.mean(refined * refined, axis=-1)
    masked = defect_mask[0].astype(jnp.float32)
    die_sum = jnp.sum(energy * masked)
    die_count = jnp.sum(masked)
    onehot = (jnp.arange(Z, dtype=jnp.int32) == my_zone).astype(jnp.float32)
    zone_sum, zone_count = lax.psum((onehot * die_sum, onehot * die_count), "col")
    zone_mean = zone_sum / jnp.maximum(zone_count, 1.0)
    mine = jnp.sum(onehot * zone_mean)
    return (energy / (mine + 0.01))[None]


def solution(mesh):
    in_specs = (
        P(("groups", "col"), None, None),
        P(("groups", "col")),
        P("groups"),
        P(("groups", "col"), None, None),
        P(),
    )
    out_specs = P(("groups", "col"), None, None)
    return jax.shard_map(body, mesh=mesh, in_specs=in_specs, out_specs=out_specs, check_vma=False)
```

profile of v0, /device:TPU:0, one launch (start us, length us, event | category | flops | bytes accessed | tf_op | source)
XLA Modules:
  0.0 422.0 jit_solution(12637861433031280978)
XLA Ops:
  11.4 42.3 %all-gather.2.cloned.1.call-done = bf16[16,8,8192]{2,1,0:T(8,128)(2,1)} async-done(((bf16[1,8,8192]{2,1,0:T(8,128)(2,1)}), bf16[16,8,8192]{2,1,0:T(8,128)(2,1)}) %all-gather.2.cloned.1.call-update) | async-done | bytes 2097168 | tf_op jit(solution)/shard_map/all_gather | solution.py:80
  53.7 2.0 select_reduce_fusion
  57.7 318.3 %while.15 = (s32[]{:T(128)}, f32[8,8192]{1,0:T(8,128)}, f32[8,128]{1,0:T(8,128)S(1)}, s32[13]{0:T(128)S(1)}, bf16[20,8960]{1,0:T(8,128)(2,1)}, /*index=5*/f32[8,...) while((s32[]{:T(128)}, f32[8,8192]{1,0:T(8,128)}, ...), condition=%wide.region_17.18_spmd.clone, body=%wide.region_3.17_spmd.clone.sunk | while | flops 3815698 | bytes 38420288 | solution.py:54
  61.1 1.3 slice_multiply_fusion.14
  62.4 1.1 reshape.317
  63.8 1.1 reshape.318
  65.2 1.1 reshape.319
  79.7 2.4 fusion.283
  85.5 1.3 slice_multiply_fusion.14
  86.8 1.1 reshape.317
  88.2 1.1 reshape.318
  89.6 1.1 reshape.319
  104.1 2.5 fusion.283
  110.0 1.3 slice_multiply_fusion.14
  111.3 1.1 reshape.317
  112.7 1.1 reshape.318
  114.1 1.1 reshape.319
  128.6 2.5 fusion.283
  134.5 1.3 slice_multiply_fusion.14
  137.2 1.1 reshape.318
  138.6 1.1 reshape.319
  153.1 2.5 fusion.283
  159.0 1.3 slice_multiply_fusion.14
  160.3 1.1 reshape.317
  161.7 1.1 reshape.318
  163.1 1.1 reshape.319
  177.6 2.5 fusion.283
  183.4 1.3 slice_multiply_fusion.14
  184.8 1.1 reshape.317
  186.1 1.1 reshape.318
  187.6 1.1 reshape.319
  202.1 2.5 fusion.283
  207.9 1.3 slice_multiply_fusion.14
  209.3 1.1 reshape.317
  210.6 1.1 reshape.318
  212.1 1.1 reshape.319
  226.6 2.5 fusion.283
  232.4 1.3 slice_multiply_fusion.14
  235.1 1.1 reshape.318
  236.6 1.1 reshape.319
  251.1 2.5 fusion.283
  256.9 1.3 slice_multiply_fusion.14
  258.3 1.1 reshape.317
  259.6 1.1 reshape.318
  261.1 1.1 reshape.319
  275.6 2.5 fusion.283
  281.4 1.3 slice_multiply_fusion.14
  284.1 1.1 reshape.318
  285.6 1.1 reshape.319
  300.1 2.5 fusion.283
  305.9 1.3 slice_multiply_fusion.14
  308.6 1.1 reshape.318
  310.1 1.1 reshape.319
  324.5 2.5 fusion.283
  330.4 1.3 slice_multiply_fusion.14
  333.1 1.1 reshape.318
  334.6 1.1 reshape.319
  349.0 2.5 fusion.283
  354.9 1.3 slice_multiply_fusion.14
  357.6 1.1 reshape.318
  359.1 1.1 reshape.319
  373.5 2.5 fusion.283
  380.5 1.3 fusion.234
  381.8 31.4 %all-reduce.30 = (f32[8]{0:T(128)S(1)}, f32[8]{0:T(128)S(1)}) all-reduce(f32[8]{0:T(128)S(1)} %get-tuple-element.221, f32[8]{0:T(128)S(1)} %get-tuple-element.220), channel_id=1, replica_groups=mesh['groups'=2,'col'=16] {'col'}, use_global_device_ids=true, to_apply=%region_20.21 | all-reduce | flops 16 | bytes 128 | tf_op jit(solution)/shard_map/psum | solution.py:96
  (974 shorter events, 214.7 us)
Async XLA Ops:
  6.5 4.8 %copy-start.3 = (bf16[1,8,8192]{2,1,0:T(8,128)(2,1)S(1)}, bf16[1,8,8192]{2,1,0:T(8,128)(2,1)}, u32[]{:S(2)}) copy-start(bf16[1,8,8192]{2,1,0:T(8,128)(2,1)} %param.7) | copy-start | bytes 393220
  6.5 2.6 copy-start.7
  6.5 4.0 copy-start.6
  6.5 47.1 %all-gather.2.cloned.1.call-start = ((), (), s32[]{:S(2)}) async-start(), calls=%async_computation | async-start | bytes 2228224 | tf_op jit(solution)/shard_map/all_gather | solution.py:80
  57.7 4.7 %copy-start = (f32[8,8192]{1,0:T(8,128)}, f32[8,8192]{1,0:T(8,128)S(1)}, u32[]{:S(2)}) copy-start(f32[8,8192]{1,0:T(8,128)S(1)} %get-tuple-element.456) | copy-start | bytes 786436 | tf_op jit(solution)/shard_map/while
  79.7 2.4 copy-start.1
  82.1 4.7 %copy-start = (f32[8,8192]{1,0:T(8,128)}, f32[8,8192]{1,0:T(8,128)S(1)}, u32[]{:S(2)}) copy-start(f32[8,8192]{1,0:T(8,128)S(1)} %get-tuple-element.456) | copy-start | bytes 786436 | tf_op jit(solution)/shard_map/while
  104.1 2.5 copy-start.1
  106.6 4.7 %copy-start = (f32[8,8192]{1,0:T(8,128)}, f32[8,8192]{1,0:T(8,128)S(1)}, u32[]{:S(2)}) copy-start(f32[8,8192]{1,0:T(8,128)S(1)} %get-tuple-element.456) | copy-start | bytes 786436 | tf_op jit(solution)/shard_map/while
  128.6 2.5 copy-start.1
  131.1 4.7 %copy-start = (f32[8,8192]{1,0:T(8,128)}, f32[8,8192]{1,0:T(8,128)S(1)}, u32[]{:S(2)}) copy-start(f32[8,8192]{1,0:T(8,128)S(1)} %get-tuple-element.456) | copy-start | bytes 786436 | tf_op jit(solution)/shard_map/while
  153.1 2.5 copy-start.1
  155.6 4.7 %copy-start = (f32[8,8192]{1,0:T(8,128)}, f32[8,8192]{1,0:T(8,128)S(1)}, u32[]{:S(2)}) copy-start(f32[8,8192]{1,0:T(8,128)S(1)} %get-tuple-element.456) | copy-start | bytes 786436 | tf_op jit(solution)/shard_map/while
  177.6 2.5 copy-start.1
  180.1 4.7 %copy-start = (f32[8,8192]{1,0:T(8,128)}, f32[8,8192]{1,0:T(8,128)S(1)}, u32[]{:S(2)}) copy-start(f32[8,8192]{1,0:T(8,128)S(1)} %get-tuple-element.456) | copy-start | bytes 786436 | tf_op jit(solution)/shard_map/while
  202.1 2.5 copy-start.1
  204.6 4.7 %copy-start = (f32[8,8192]{1,0:T(8,128)}, f32[8,8192]{1,0:T(8,128)S(1)}, u32[]{:S(2)}) copy-start(f32[8,8192]{1,0:T(8,128)S(1)} %get-tuple-element.456) | copy-start | bytes 786436 | tf_op jit(solution)/shard_map/while
  226.6 2.5 copy-start.1
  229.1 4.7 %copy-start = (f32[8,8192]{1,0:T(8,128)}, f32[8,8192]{1,0:T(8,128)S(1)}, u32[]{:S(2)}) copy-start(f32[8,8192]{1,0:T(8,128)S(1)} %get-tuple-element.456) | copy-start | bytes 786436 | tf_op jit(solution)/shard_map/while
  251.1 2.5 copy-start.1
  253.6 4.7 %copy-start = (f32[8,8192]{1,0:T(8,128)}, f32[8,8192]{1,0:T(8,128)S(1)}, u32[]{:S(2)}) copy-start(f32[8,8192]{1,0:T(8,128)S(1)} %get-tuple-element.456) | copy-start | bytes 786436 | tf_op jit(solution)/shard_map/while
  275.6 2.5 copy-start.1
  278.1 4.7 %copy-start = (f32[8,8192]{1,0:T(8,128)}, f32[8,8192]{1,0:T(8,128)S(1)}, u32[]{:S(2)}) copy-start(f32[8,8192]{1,0:T(8,128)S(1)} %get-tuple-element.456) | copy-start | bytes 786436 | tf_op jit(solution)/shard_map/while
  300.1 2.5 copy-start.1
  302.6 4.7 %copy-start = (f32[8,8192]{1,0:T(8,128)}, f32[8,8192]{1,0:T(8,128)S(1)}, u32[]{:S(2)}) copy-start(f32[8,8192]{1,0:T(8,128)S(1)} %get-tuple-element.456) | copy-start | bytes 786436 | tf_op jit(solution)/shard_map/while
  324.5 2.5 copy-start.1
  327.1 4.7 %copy-start = (f32[8,8192]{1,0:T(8,128)}, f32[8,8192]{1,0:T(8,128)S(1)}, u32[]{:S(2)}) copy-start(f32[8,8192]{1,0:T(8,128)S(1)} %get-tuple-element.456) | copy-start | bytes 786436 | tf_op jit(solution)/shard_map/while
  349.0 2.5 copy-start.1
  351.6 4.7 %copy-start = (f32[8,8192]{1,0:T(8,128)}, f32[8,8192]{1,0:T(8,128)S(1)}, u32[]{:S(2)}) copy-start(f32[8,8192]{1,0:T(8,128)S(1)} %get-tuple-element.456) | copy-start | bytes 786436 | tf_op jit(solution)/shard_map/while
  373.5 2.5 copy-start.1
  376.0 1.0 copy-start.2
  376.0 1.0 copy-start.4
  377.5 0.9 copy-start.5
Sparse Core Ops, SparseCore 0:
  9.5 44.0 all-gather.1
where the time goes:
time: 425 us; the launch traced here: 422 us
  local copies, waits for them, and re-layouts  179 us (42%)
  other arithmetic  125 us (29%)
  waiting for transfers between devices  43 us (10%)
  blocking collectives  31.4 us (7%)
  loops' own time  27.6 us (6%)
  between operations  15 us (4%)
    reshape x170, local copies, waits for them, and re-layouts, channel_sum(): return jnp.sum(values.reshape(values.shape[0], -1, chans), axis=-1)  73.2 us
    reshape x169, local copies, waits for them, and re-layouts, row_step(): numer = numer + jnp.repeat(expo, chans, axis=1) * moved  59 us
    all_gather x1, waiting for transfers between devices, body(): piece = lax.all_gather(features, 'col', axis=0, tiled=True)  42.3 us
    reduce_sum x171, other arithmetic, channel_sum(): return jnp.sum(values.reshape(values.shape[0], -1, chans), axis=-1)  35.9 us
    add x13, other arithmetic, row_step(): numer = numer + jnp.repeat(expo, chans, axis=1) * moved  32.5 us
    broadcast_in_dim x169, local copies, waits for them, and re-layouts, row_step(): numer = numer + jnp.repeat(expo, chans, axis=1) * moved  32.3 us
    psum x1, blocking collectives, body(): lax.psum((onehot * die_sum, onehot * die_count), 'col')  31.4 us
    another operation x1, loops' own time, align_golden(): lax.scan(row_step, start, jnp.arange(side, dtype=jnp.int32))  27.6 us
  transfers between devices with their start and end apart: 1, of which 1 were waited for; matrix products, arithmetic and copies ran while one was open for 1% of the time, Pallas kernels for 0%

commit v1 on v0

v1 whole, which is shorter than its diff:
```python
import functools

import jax
import jax.numpy as jnp
from jax import lax
from jax.experimental import pallas as pl
from jax.experimental.pallas import tpu as pltpu
from jax.sharding import PartitionSpec as P

C = 64
SHIFT = 6
BOX = 5
Z = 8
SIDE = 2 * SHIFT + 1
REACH = BOX // 2
HALO = SHIFT + REACH + 2
ROWS = 8
SLOT = 16
TOP = (SLOT - ROWS) // 2
LANES = 128
LOG2E = 1.4426950408889634
F32 = jnp.float32
BF16 = jnp.bfloat16


def iota(shape, dim):
    return lax.broadcasted_iota(jnp.int32, shape, dim)


def pack_kernel(chips, w, zone_ref, feat_ref, mask_ref, out_ref):
    width = mask_ref.shape[2]
    half = (w + 2 * HALO) // 2
    zone = zone_ref[0].astype(F32)
    mask = mask_ref[0].astype(F32)
    lane = iota((ROWS, LANES), 1)
    for p in range(chips):
        for t in range(half // 2):
            parts = []
            for part in range(2):
                col = p * w - HALO + part * half + 2 * t
                if 0 <= col < width:
                    parts.append(feat_ref[0, :, col * C : (col + 2) * C].astype(F32))
                else:
                    parts.append(jnp.zeros((ROWS, LANES), F32))
            out_ref[p, :, t * LANES : (t + 1) * LANES] = jnp.concatenate(parts, 0).astype(BF16)
        here = pltpu.roll(mask, (width - p * w) % width, 1) if p else mask
        here = jnp.where(lane < w, here, 0.0)
        last = jnp.concatenate([here, jnp.full((ROWS, LANES), 1.0, F32) * zone], 0)
        out_ref[p, :, half // 2 * LANES :] = last.astype(BF16)


def main_kernel(
    chips, w, me_ref, owner_ref, own_ref, other_ref, kern_ref, out_ref,
    pad_ref, test_ref, gold_ref, goldc_ref, goldsq_ref, self_ref, res_ref, hid_ref,
):
    cols = w + 2 * HALO
    half = cols // 2
    raw = w + 4 + 2 * REACH
    outs = w + 4
    me = me_ref[0]
    chip = me // 2
    core = me % 2
    not_first = jnp.where(chip == 0, 0.0, 1.0).astype(F32)
    not_last = jnp.where(chip == chips - 1, 0.0, 1.0).astype(F32)

    lane8 = iota((ROWS, LANES), 1)
    sub8 = iota((ROWS, LANES), 0)
    low8 = lane8 < C
    low16 = iota((SLOT, LANES), 1) < C
    ones = jnp.ones((LANES, LANES), BF16)
    ones2 = jnp.ones((2 * LANES, LANES), BF16)

    twice = (iota((C, LANES), 1) % C == iota((C, LANES), 0)).astype(BF16)
    weights = []
    for conv in range(2):
        doubled = jnp.dot(kern_ref[conv], twice, preferred_element_type=F32).astype(BF16)
        by_col = []
        for dx in range(3):
            taps = [doubled[(3 * dy + dx) * C : (3 * dy + dx + 1) * C] for dy in range(3)]
            by_col.append(jnp.concatenate(taps + [jnp.zeros((C, LANES), BF16)], 0))
        weights.append(jnp.concatenate(by_col, 1))

    spread_r = iota((LANES, 2 * LANES), 0)
    spread_c = iota((LANES, 2 * LANES), 1)
    spread = ((spread_c // LANES == spread_r // C) & (spread_c % C == spread_r % C)).astype(BF16)
    zero8 = jnp.zeros((ROWS, LANES), F32)
    for which, src in enumerate((own_ref, other_ref)):

        def unpack(i, carry, src=src, base=which * chips):
            for g in range(cols + 1):
                pad_ref[base + i, g * SLOT : g * SLOT + ROWS, :] = zero8
            for t in range(half // 2):
                both = jnp.dot(src[i, :, t * LANES : (t + 1) * LANES], spread, preferred_element_type=F32)
                for part in range(2):
                    for odd in range(2):
                        row = (part * half + 2 * t + odd) * SLOT + ROWS
                        pad_ref[base + i, row : row + ROWS, :] = both[
                            part * ROWS : (part + 1) * ROWS, odd * LANES : (odd + 1) * LANES
                        ]
            return carry

        lax.fori_loop(0, chips, unpack, 0)

    for ref, count in ((self_ref, outs), (res_ref, outs), (hid_ref, w + 2)):
        for i in range(count + 1):
            ref[i * SLOT : i * SLOT + ROWS, :] = zero8
    goldsq_ref[cols * SLOT :, :] = jnp.zeros((goldsq_ref.shape[0] - cols * SLOT, LANES), BF16)

    lane_w = iota((ROWS, 2 * LANES), 1)
    sub_w = iota((ROWS, 2 * LANES), 0)
    valid = []
    for k in range(4):
        b = lane_w // SLOT - k
        a = lane_w % SLOT - TOP - sub_w
        valid.append((b >= 0) & (b < SIDE) & (jnp.abs(a) <= SHIFT))
    outside = jnp.maximum(SHIFT - TOP - sub8, 0) + jnp.maximum(sub8 + SHIFT - (SLOT - TOP - 1), 0)
    outside = (outside * SIDE).astype(F32)

    lanes_g = goldsq_ref.shape[0]
    sub_g = iota((ROWS, lanes_g), 0)

    def split_square(values, low):
        square = values * values
        high = square.astype(BF16).astype(F32)
        return jnp.where(low, high, square - high).astype(BF16)

    def one_die(i, zones):
        tail = own_ref[i, :, half // 2 * LANES :].astype(F32)
        mask = tail[:ROWS]
        zone = tail[ROWS, 0].astype(jnp.int32)
        owner = owner_ref[zone]
        gold = owner // 2 + jnp.where(owner % 2 == core, 0, chips)

        for g in range(cols):
            rows = [pad_ref[gold, g * SLOT + TOP + dy : g * SLOT + TOP + dy + SLOT, :] for dy in range(-2, 3)]
            at = slice(g * SLOT, (g + 1) * SLOT)
            gold_ref[at, 0:LANES] = jnp.where(low16, rows[0], rows[1]).astype(BF16)
            gold_ref[at, LANES : 2 * LANES] = jnp.where(low16, rows[2], rows[3]).astype(BF16)
            gold_ref[at, 2 * LANES :] = rows[4].astype(BF16)
            goldc_ref[at, :] = rows[2].astype(BF16)
            goldsq_ref[at, :] = split_square(rows[2], low16)
        squares = []
        for r in range(0, raw, 2):
            tiles = [[], [], []]
            centre = []
            for q in (r, r + 1):
                base = (q + HALO - REACH - 2) * SLOT + ROWS
                rows = [pad_ref[i, base + dy : base + dy + ROWS, :] for dy in range(-2, 3)]
                tiles[0].append(jnp.where(low8, rows[0], rows[1]))
                tiles[1].append(jnp.where(low8, rows[2], rows[3]))
                tiles[2].append(jnp.where(low8, rows[4], 0.0))
                centre.append(rows[2])
            at = slice(r * ROWS, (r + 2) * ROWS)
            for t in range(3):
                test_ref[at, t * LANES : (t + 1) * LANES] = jnp.concatenate(tiles[t], 0).astype(BF16)
            squares.append(split_square(jnp.concatenate(centre, 0), low16))

        energy = jnp.dot(jnp.concatenate(squares, 0), ones, preferred_element_type=F32)
        energy = [energy[r * ROWS : (r + 1) * ROWS] for r in range(raw)]
        for l in range(outs):
            self_ref[l * SLOT + ROWS : (l + 1) * SLOT, :] = sum(energy[l + 1 : l + BOX], energy[l])
        self_box = []
        for l in range(outs):
            base = l * SLOT + ROWS
            rows = [self_ref[base + dy : base + dy + ROWS, :] for dy in range(-2, 3)]
            self_box.append(sum(rows[1:], rows[0]))

        e = lax.dot_general(
            jnp.ones((SLOT, LANES), BF16), goldsq_ref[...], (((1,), (1,)), ((), ())), preferred_element_type=F32
        )[:ROWS]
        down = e
        for dy in (-2, -1, 1, 2):
            inside = (sub_g + dy >= 0) & (sub_g + dy < ROWS)
            down = down + jnp.where(inside, pltpu.roll(e, (-dy) % lanes_g, 1), 0.0)
        moved = [down] + [pltpu.roll(down, lanes_g - SLOT * d, 1) for d in range(1, BOX)]
        whole = sum(moved[1:], moved[0])
        edge = {
            2: moved[2] + moved[3] + moved[4] + not_first * (moved[0] + moved[1]),
            3: moved[1] + moved[2] + moved[3] + moved[4] + not_first * moved[0],
            w: moved[0] + moved[1] + moved[2] + moved[3] + not_last * moved[4],
            w + 1: moved[0] + moved[1] + moved[2] + not_last * (moved[3] + moved[4]),
        }
        whole_by = (whole, pltpu.roll(whole, lanes_g - C, 1))
        edge = {l: pltpu.roll(v, lanes_g - C, 1) if (l // 4) % 2 else v for l, v in edge.items()}

        sheared = []
        for j in range(raw // 4):
            block = lax.dot_general(
                test_ref[4 * j * ROWS : 4 * (j + 1) * ROWS, :],
                gold_ref[4 * j * SLOT : (4 * j + 16) * SLOT, :],
                (((1,), (1,)), ((), ())),
                preferred_element_type=F32,
            )
            for k in range(4):
                row = block[k * ROWS : (k + 1) * ROWS]
                sheared.append(pltpu.roll(row, 2 * LANES - k * SLOT, 1) if k else row)
        pairs = [sheared[r] + sheared[r + 1] for r in range(raw - 1)]
        res = []
        for m in range(outs // 4):
            chosen = []
            for k in range(4):
                l = 4 * m + k
                cross = pairs[l] + pairs[l + 2] + sheared[l + 4]
                cross = pltpu.roll(cross, k * SLOT, 1) if k else cross
                src = edge.get(l, whole_by[m % 2])
                at = (m - m % 2) * C
                scale = lax.rsqrt(jnp.concatenate([self_box[l]] * 2, 1) * src[:, at : at + 2 * LANES] + 1e-05)
                expo = jnp.exp2((32.0 * LOG2E) * cross * scale)
                chosen.append(jnp.where(valid[k], expo, 0.0))
            weight = jnp.concatenate(chosen, 0).astype(BF16)
            at = (4 * m + 2) * SLOT
            numer = jnp.dot(weight, goldc_ref[at : at + 16 * SLOT, :], preferred_element_type=F32)
            denom = jnp.dot(weight, ones2, preferred_element_type=F32)
            for k in range(4):
                l = 4 * m + k
                at = slice(k * ROWS, (k + 1) * ROWS)
                base = (l + HALO - 2) * SLOT + ROWS
                value = pad_ref[i, base : base + ROWS, :] - numer[at] / (denom[at] + outside)
                if l < 2:
                    value = value * not_first
                if l >= w + 2:
                    value = value * not_last
                value = value.astype(BF16).astype(F32)
                res.append(value)
                res_ref[l * SLOT + ROWS : (l + 1) * SLOT, :] = value

        def convolve(ref, count, weight):
            first, second = [], []
            for l in range(count):
                base = l * SLOT + ROWS
                first.append(jnp.where(low8, ref[base - 1 : base - 1 + ROWS, :], ref[base : base + ROWS, :]))
                second.append(ref[base + 1 : base + 1 + ROWS, :])
            rows = jnp.concatenate([jnp.concatenate(first, 0), jnp.concatenate(second, 0)], 1).astype(BF16)
            full = jnp.dot(rows, weight, preferred_element_type=F32)
            full = [full[l * ROWS : (l + 1) * ROWS] for l in range(count)]
            return [
                full[x][:, :LANES] + full[x + 1][:, LANES : 2 * LANES] + full[x + 2][:, 2 * LANES :]
                for x in range(count - 2)
            ]

        for h, value in enumerate(convolve(res_ref, outs, weights[0])):
            value = jnp.maximum(value, 0.0).astype(BF16).astype(F32)
            if h == 0:
                value = value * not_first
            if h == w + 1:
                value = value * not_last
            hid_ref[h * SLOT + ROWS : (h + 1) * SLOT, :] = value
        found = jnp.zeros((ROWS, LANES), F32)
        for x, value in enumerate(convolve(hid_ref, w + 2, weights[1])):
            refined = res[x + 2] + value
            mean = jnp.sum(refined * refined, axis=1, keepdims=True) * (1.0 / LANES)
            found = jnp.where(lane8 == x, mean, found)

        out_ref[2 * i + core] = found
        out_ref[2 * i + 1 - core] = jnp.zeros((ROWS, LANES), F32)
        mask = jnp.where(lane8 < w, mask, 0.0)
        total = jnp.sum(jnp.sum(found * mask, axis=1, keepdims=True), axis=0, keepdims=True)
        count = jnp.sum(jnp.sum(mask, axis=1, keepdims=True), axis=0, keepdims=True)
        here = sub8 == zone
        zones = zones + jnp.where(here & (lane8 == w), total, 0.0)
        return zones + jnp.where(here & (lane8 == w + 1), count, 0.0)

    zones = lax.fori_loop(0, chips, one_die, jnp.zeros((ROWS, LANES), F32))
    for d in range(2 * chips):
        out_ref[d] = out_ref[d] + zones


def score_kernel(chips, w, zone_ref, back_ref, out_ref):
    lane = iota((ROWS, LANES), 1)
    sub = iota((ROWS, LANES), 0)
    total = back_ref[0]
    for d in range(1, 2 * chips):
        total = total + back_ref[d]
    mine = jnp.where(sub == zone_ref[0], total, 0.0)
    zone_sum = jnp.sum(jnp.sum(jnp.where(lane == w, mine, 0.0), axis=1, keepdims=True), axis=0, keepdims=True)
    zone_count = jnp.sum(jnp.sum(jnp.where(lane == w + 1, mine, 0.0), axis=1, keepdims=True), axis=0, keepdims=True)
    zone_mean = zone_sum / jnp.maximum(zone_count, 1.0)
    energy = jnp.zeros((ROWS, LANES), F32)
    for p in range(chips):
        strip = back_ref[2 * p] + back_ref[2 * p + 1]
        strip = pltpu.roll(strip, p * w, 1) if p else strip
        energy = jnp.where((lane >= p * w) & (lane < (p + 1) * w), strip, energy)
    out_ref[0] = energy / (zone_mean + 0.01)


def body(n, features, zone_ids, golden_owner, defect_mask, kernels):
    chips = n // 2
    w = defect_mask.shape[2] // chips
    cols = w + 2 * HALO
    raw = w + 4 + 2 * REACH
    outs = w + 4
    half = cols // 2
    length = half * C + LANES
    smem = pl.BlockSpec(memory_space=pltpu.SMEM)
    vmem = pl.BlockSpec(memory_space=pltpu.VMEM)
    params = pltpu.CompilerParams(vmem_limit_bytes=48 * 2**20)

    packed = pl.pallas_call(
        functools.partial(pack_kernel, chips, w),
        out_shape=jax.ShapeDtypeStruct((chips, 2 * ROWS, length), BF16),
        in_specs=[smem, vmem, vmem],
        out_specs=vmem,
        compiler_params=params,
    )(zone_ids, features, defect_mask)
    groups = [[2 * p + c for p in range(chips)] for c in range(2)]
    own = lax.all_to_all(packed, "col", 0, 0, axis_index_groups=groups, tiled=True)
    other = lax.ppermute(own, "col", [(d, d ^ 1) for d in range(n)])
    me = lax.axis_index("col").astype(jnp.int32).reshape(1)
    lanes_g = -(-cols * SLOT // LANES) * LANES
    partial = pl.pallas_call(
        functools.partial(main_kernel, chips, w),
        out_shape=jax.ShapeDtypeStruct((n, ROWS, LANES), F32),
        in_specs=[smem, smem, vmem, vmem, vmem],
        out_specs=vmem,
        scratch_shapes=[
            pltpu.VMEM((n, cols * SLOT + ROWS, LANES), F32),
            pltpu.VMEM((raw * ROWS, 3 * LANES), BF16),
            pltpu.VMEM((cols * SLOT, 3 * LANES), BF16),
            pltpu.VMEM((cols * SLOT, LANES), BF16),
            pltpu.VMEM((lanes_g, LANES), BF16),
            pltpu.VMEM((outs * SLOT + ROWS, LANES), F32),
            pltpu.VMEM((outs * SLOT + ROWS, LANES), F32),
            pltpu.VMEM(((w + 2) * SLOT + ROWS, LANES), F32),
        ],
        compiler_params=params,
    )(me, golden_owner, own, other, kernels)
    back = lax.all_to_all(partial, "col", 0, 0, tiled=True)
    return pl.pallas_call(
        functools.partial(score_kernel, chips, w),
        out_shape=jax.ShapeDtypeStruct(defect_mask.shape, F32),
        in_specs=[smem, vmem],
        out_specs=vmem,
        compiler_params=params,
    )(zone_ids, back)


def solution(mesh):
    split = P(("groups", "col"), None, None)
    return jax.shard_map(
        functools.partial(body, mesh.shape["col"]),
        mesh=mesh,
        in_specs=(split, P(("groups", "col")), P("groups"), split, P()),
        out_specs=split,
        check_vma=False,
    )
```

time: 425 us -> 48 us (0.11)
  local copies, waits for them, and re-layouts: 179 us -> 1.79 us
  other arithmetic: 125 us -> 0 us
  waiting for transfers between devices: 43 us -> 1.42 us
  loops' own time: 27.6 us -> 0 us
  Pallas kernels: 0 us -> 15.9 us
  between operations: 15 us -> 0.68 us
    reshape x342 -> x0, local copies, waits for them, and re-layouts: 133 us -> none  [the longest x170 73.2 us: channel_sum(): return jnp.sum(values.reshape(values.shape[0], -1, chans), axis=-1)]
    add x197 -> x0, other arithmetic: 51.4 us -> none  [the longest x13 32.5 us: row_step(): numer = numer + jnp.repeat(expo, chans, axis=1) * moved]
    all_gather x1 -> x0, waiting for transfers between devices: 42.3 us -> none  [body(): piece = lax.all_gather(features, 'col', axis=0, tiled=True)]
    reduce_sum x175 -> x0, other arithmetic: 39.7 us -> none  [the longest x171 35.9 us: channel_sum(): return jnp.sum(values.reshape(values.shape[0], -1, chans), axis=-1)]
    broadcast_in_dim x170 -> x0, local copies, waits for them, and re-layouts: 32.5 us -> none  [the longest x169 32.3 us: row_step(): numer = numer + jnp.repeat(expo, chans, axis=1) * moved]
    psum x1 -> x0, blocking collectives: 31.4 us -> none  [body(): lax.psum((onehot * die_sum, onehot * die_count), 'col')]
    all_to_all x0 -> x2, blocking collectives: none -> 27.9 us  [the longest x1 18.1 us: body(): lax.all_to_all(packed, 'col', 0, 0, axis_index_groups=groups, tiled=True)]
    another operation x1 -> x0, loops' own time: 27.6 us -> none  [align_golden(): lax.scan(row_step, start, jnp.arange(side, dtype=jnp.int32))]
  transfers between devices with their start and end apart: 1 -> 1, of which waited for: 1 -> 1; matrix products, arithmetic and copies ran while one was open for 1% -> 0% of each run, Pallas kernels for 0% -> 0%
where the time goes in v1:
time: 48 us; the launch traced here: 47.7 us
  blocking collectives  27.9 us (58%)
  Pallas kernels  15.9 us (33%)
  local copies, waits for them, and re-layouts  1.79 us (4%)
  waiting for transfers between devices  1.42 us (3%)
  between operations  0.68 us (1%)
    all_to_all x1, blocking collectives, body(): lax.all_to_all(packed, 'col', 0, 0, axis_index_groups=groups, tiled=True)  18.1 us
    pallas_call x1, Pallas kernels, body(): pl.pallas_call(functools.partial(main_kernel, chips, w), out_shape=jax.Sh...  15.2 us
    all_to_all x1, blocking collectives, body(): back = lax.all_to_all(partial, 'col', 0, 0, tiled=True)  9.8 us
    unnamed x9, local copies, waits for them, and re-layouts  1.79 us
    ppermute x1, waiting for transfers between devices, body(): other = lax.ppermute(own, 'col', [(d, d ^ 1) for d in range(n)])  1.42 us
  transfers between devices with their start and end apart: 1, of which 1 were waited for; matrix products, arithmetic and copies ran while one was open for 0% of the time, Pallas kernels for 0%

profile of v1, /device:TPU:0, one launch (start us, length us, event | category | flops | bytes accessed | tf_op | source)
XLA Modules:
  0.0 47.7 jit_solution(16665161239140129169)
XLA Ops:
  0.7 0.0 copy-start
  0.7 0.9 %copy-done = bf16[1,8,8192]{2,1,0:T(8,128)(2,1)S(1)} copy-done((bf16[1,8,8192]{2,1,0:T(8,128)(2,1)S(1)}, bf16[1,8,8192]{2,1,0:T(8,128)(2,1)}, u32[]{:S(2)}) %copy-start) | copy-done | bytes 131096
  1.6 0.0 copy-start.1
  1.6 0.7 %copy-done.1 = s32[1,8,128]{2,1,0:T(8,128)S(1)} copy-done((s32[1,8,128]{2,1,0:T(8,128)S(1)}, s32[1,8,128]{2,1,0:T(8,128)}, u32[]{:S(2)}) %copy-start.1) | copy-done | bytes 4120
  2.2 0.1 shard_map.55
  2.3 0.0 copy-start.3
  2.3 18.1 %all_to_all.10.own_ref = bf16[8,16,1280]{2,1,0:T(8,128)(2,1)S(1)} all-to-all(bf16[8,16,1280]{2,1,0:T(8,128)(2,1)S(1)} %shard_map.55), channel_id=1, replica_groups={{0,2,4,6,8,10,12,14},{1,3,5,7,9,11,13,15},{16,18,20,22,24,26,28,30},{17..., dimensions={0} | all-to-all | bytes 655360 | tf_op jit(solution)/shard_map/all_to_all | solution.py:306
  20.4 0.0 collective-permute-start
  20.5 0.0 copy-done.3
  20.5 0.2 copy.6.kern_ref
  20.6 0.0 copy-start.2
  20.7 1.4 %collective-permute-done.other_ref = bf16[8,16,1280]{2,1,0:T(8,128)(2,1)S(1)} collective-permute-done((bf16[8,16,1280]{2,1,0:T(8,128)(2,1)S(1)}, bf16[8,16,1280]{2,1,0:T(8,128)(2,1)S(1)}, u32[]{:S(2)}, u32[]{:S(2)}) %collective-permute-start) | collective-permute-done | bytes 327712 | tf_op jit(solution)/shard_map/ppermute | solution.py:307
  22.1 0.0 copy-done.2
  22.1 15.2 %shard_map.56 = f32[16,8,128]{2,1,0:T(8,128)S(1)} custom-call(s32[1]{0:T(128)} %bitcast.me_ref, s32[8]{0:T(128)S(1)} %copy-done.2, bf16[8,16,1280]{2,1,0:T(8,128)(2,1)S(1)} %all_to_all.10.own_ref, bf16[8,16,1280]{2,1,0:T(8,128)(2,1)S(1)} %collective-permute-done.other_ref, bf16[2,576,64]{2,1,0:T(8,128)(2,1)S(1)} %copy.6.kern_ref), custom_call_target="tpu_custom_call" | custom-call | tf_op jit(solution)/shard_map/pallas_call | solution.py:310
  37.2 9.8 %all_to_all.11.back_ref = f32[16,8,128]{2,1,0:T(8,128)S(1)} all-to-all(f32[16,8,128]{2,1,0:T(8,128)S(1)} %shard_map.56), channel_id=1, replica_groups=mesh['groups'=2,'col'=16] {'col'}, dimensions={0} | all-to-all | bytes 131072 | tf_op jit(solution)/shard_map/all_to_all | solution.py:327
  47.0 0.7 %shard_map.57 = f32[1,8,128]{2,1,0:T(8,128)} custom-call(s32[1]{0:T(128)S(6)} %copy.7.zone_ref, f32[16,8,128]{2,1,0:T(8,128)S(1)} %all_to_all.11.back_ref), custom_call_target="tpu_custom_call" | custom-call | tf_op jit(solution)/shard_map/pallas_call | solution.py:328
Async XLA Ops:
  0.7 0.9 %copy-start = (bf16[1,8,8192]{2,1,0:T(8,128)(2,1)S(1)}, bf16[1,8,8192]{2,1,0:T(8,128)(2,1)}, u32[]{:S(2)}) copy-start(bf16[1,8,8192]{2,1,0:T(8,128)(2,1)} %feat_ref.1) | copy-start | bytes 393220
  1.6 0.7 %copy-start.1 = (s32[1,8,128]{2,1,0:T(8,128)S(1)}, s32[1,8,128]{2,1,0:T(8,128)}, u32[]{:S(2)}) copy-start(s32[1,8,128]{2,1,0:T(8,128)} %mask_ref.1) | copy-start | bytes 12292
  2.3 18.1 %copy-start.3 = (bf16[2,576,64]{1,2,0:T(8,128)(2,1)S(1)}, bf16[2,576,64]{1,2,0:T(8,128)(2,1)}, u32[]{:S(2)}) copy-start(bf16[2,576,64]{1,2,0:T(8,128)(2,1)} %param.9) | copy-start | bytes 442372
  20.4 1.6 %collective-permute-start = (bf16[8,16,1280]{2,1,0:T(8,128)(2,1)S(1)}, bf16[8,16,1280]{2,1,0:T(8,128)(2,1)S(1)}, u32[]{:S(2)}, u32[]{:S(2)}) collective-permute-start(bf16[8,16,1280]{2,1,0:T(8,128)(2,1)S(1)} %all_to_all.10.own_ref), channel_id=1, source_target_pairs={{0,1},{1,0},{2,3},{3,2},{4,5},{5,4},{6,7},{7,6},{8,9},{9,8},{10,11... | collective-permute-start | bytes 983048 | tf_op jit(solution)/shard_map/ppermute | solution.py:307
  20.6 1.4 %copy-start.2 = (s32[8]{0:T(128)S(1)}, s32[8]{0:T(128)}, u32[]{:S(2)}) copy-start(s32[8]{0:T(128)} %owner_ref.1) | copy-start | bytes 100

commit v2 on v1

--- a/solution.py
+++ b/solution.py
@@ -18,6 +18,7 @@
 SLOT = 16
 TOP = (SLOT - ROWS) // 2
 LANES = 128
+PAIR = 4
 LOG2E = 1.4426950408889634
 F32 = jnp.float32
 BF16 = jnp.bfloat16
@@ -50,8 +51,7 @@
 
 
 def main_kernel(
-    chips, w, me_ref, owner_ref, own_ref, other_ref, kern_ref, out_ref,
-    pad_ref, test_ref, gold_ref, goldc_ref, goldsq_ref, self_ref, res_ref, hid_ref,
+    chips, w, me_ref, owner_ref, own_ref, other_ref, kern_ref, out_ref, res_ref, hid_ref, *scratch
 ):
     cols = w + 2 * HALO
     half = cols // 2
@@ -69,6 +69,7 @@
     low16 = iota((SLOT, LANES), 1) < C
     ones = jnp.ones((LANES, LANES), BF16)
     ones2 = jnp.ones((2 * LANES, LANES), BF16)
+    zero8 = jnp.zeros((ROWS, LANES), F32)
 
     twice = (iota((C, LANES), 1) % C == iota((C, LANES), 0)).astype(BF16)
     weights = []
@@ -80,31 +81,24 @@
             by_col.append(jnp.concatenate(taps + [jnp.zeros((C, LANES), BF16)], 0))
         weights.append(jnp.concatenate(by_col, 1))
 
-    spread_r = iota((LANES, 2 * LANES), 0)
-    spread_c = iota((LANES, 2 * LANES), 1)
-    spread = ((spread_c // LANES == spread_r // C) & (spread_c % C == spread_r % C)).astype(BF16)
-    zero8 = jnp.zeros((ROWS, LANES), F32)
-    for which, src in enumerate((own_ref, other_ref)):
-
-        def unpack(i, carry, src=src, base=which * chips):
-            for g in range(cols + 1):
-                pad_ref[base + i, g * SLOT : g * SLOT + ROWS, :] = zero8
-            for t in range(half // 2):
-                both = jnp.dot(src[i, :, t * LANES : (t + 1) * LANES], spread, preferred_element_type=F32)
-                for part in range(2):
-                    for odd in range(2):
-                        row = (part * half + 2 * t + odd) * SLOT + ROWS
-                        pad_ref[base + i, row : row + ROWS, :] = both[
-                            part * ROWS : (part + 1) * ROWS, odd * LANES : (odd + 1) * LANES
-                        ]
-            return carry
-
-        lax.fori_loop(0, chips, unpack, 0)
-
-    for ref, count in ((self_ref, outs), (res_ref, outs), (hid_ref, w + 2)):
-        for i in range(count + 1):
-            ref[i * SLOT : i * SLOT + ROWS, :] = zero8
-    goldsq_ref[cols * SLOT :, :] = jnp.zeros((goldsq_ref.shape[0] - cols * SLOT, LANES), BF16)
+    zones, golds = [], []
+    for i in range(chips):
+        zone = own_ref[i, :, half // 2 * LANES :].astype(F32)[ROWS, 0].astype(jnp.int32)
+        zones.append(zone)
+        golds.append(owner_ref[zone])
+
+    def pick(values, step, u):
+        found = values[u]
+        for i in range(1, chips // PAIR):
+            found = jnp.where(step == i, values[PAIR * i + u], found)
+        return found
+
+    for u in range(PAIR):
+        gpad_ref, tpad_ref, _, _, _, goldsq_ref, self_ref = scratch[7 * u : 7 * u + 7]
+        for ref, count in ((gpad_ref, cols), (tpad_ref, raw), (self_ref, outs)):
+            for i in range(count + 1):
+                ref[i * SLOT : i * SLOT + ROWS, :] = zero8
+        goldsq_ref[cols * SLOT :, :] = jnp.zeros((goldsq_ref.shape[0] - cols * SLOT, LANES), BF16)
 
     lane_w = iota((ROWS, 2 * LANES), 1)
     sub_w = iota((ROWS, 2 * LANES), 0)
@@ -116,7 +110,7 @@
     outside = jnp.maximum(SHIFT - TOP - sub8, 0) + jnp.maximum(sub8 + SHIFT - (SLOT - TOP - 1), 0)
     outside = (outside * SIDE).astype(F32)
 
-    lanes_g = goldsq_ref.shape[0]
+    lanes_g = scratch[5].shape[0]
     sub_g = iota((ROWS, lanes_g), 0)
 
     def split_square(values, low):
@@ -124,15 +118,31 @@
         high = square.astype(BF16).astype(F32)
         return jnp.where(low, high, square - high).astype(BF16)
 
-    def one_die(i, zones):
-        tail = own_ref[i, :, half // 2 * LANES :].astype(F32)
-        mask = tail[:ROWS]
-        zone = tail[ROWS, 0].astype(jnp.int32)
-        owner = owner_ref[zone]
-        gold = owner // 2 + jnp.where(owner % 2 == core, 0, chips)
-
+    def spread(tile):
+        tile = tile.astype(F32)
+        found = []
+        for part in range(2):
+            here = tile[part * ROWS : (part + 1) * ROWS]
+            turned = pltpu.roll(here, C, 1)
+            found.append((jnp.where(low8, here, turned), jnp.where(low8, turned, here)))
+        return found
+
+    def align(i, owner, gpad_ref, tpad_ref, test_ref, gold_ref, goldc_ref, goldsq_ref, self_ref):
+        mine = owner % 2 == core
+        for t in range(half // 2):
+            at = slice(t * LANES, (t + 1) * LANES)
+            tile = jnp.where(mine, own_ref[owner // 2, :, at], other_ref[owner // 2, :, at])
+            for part, both in enumerate(spread(tile)):
+                for odd, value in enumerate(both):
+                    row = (part * half + 2 * t + odd) * SLOT + ROWS
+                    gpad_ref[row : row + ROWS, :] = value
+            for part, both in enumerate(spread(own_ref[i, :, at])):
+                for odd, value in enumerate(both):
+                    r = part * half + 2 * t + odd - (HALO - REACH - 2)
+                    if 0 <= r < raw:
+                        tpad_ref[r * SLOT + ROWS : (r + 1) * SLOT, :] = value
         for g in range(cols):
-            rows = [pad_ref[gold, g * SLOT + TOP + dy : g * SLOT + TOP + dy + SLOT, :] for dy in range(-2, 3)]
+            rows = [gpad_ref[g * SLOT + TOP + dy : g * SLOT + TOP + dy + SLOT, :] for dy in range(-2, 3)]
             at = slice(g * SLOT, (g + 1) * SLOT)
             gold_ref[at, 0:LANES] = jnp.where(low16, rows[0], rows[1]).astype(BF16)
             gold_ref[at, LANES : 2 * LANES] = jnp.where(low16, rows[2], rows[3]).astype(BF16)
@@ -144,8 +154,8 @@
             tiles = [[], [], []]
             centre = []
             for q in (r, r + 1):
-                base = (q + HALO - REACH - 2) * SLOT + ROWS
-                rows = [pad_ref[i, base + dy : base + dy + ROWS, :] for dy in range(-2, 3)]
+                base = q * SLOT + ROWS
+                rows = [tpad_ref[base + dy : base + dy + ROWS, :] for dy in range(-2, 3)]
                 tiles[0].append(jnp.where(low8, rows[0], rows[1]))
                 tiles[1].append(jnp.where(low8, rows[2], rows[3]))
                 tiles[2].append(jnp.where(low8, rows[4], 0.0))
@@ -195,7 +205,6 @@
                 row = block[k * ROWS : (k + 1) * ROWS]
                 sheared.append(pltpu.roll(row, 2 * LANES - k * SLOT, 1) if k else row)
         pairs = [sheared[r] + sheared[r + 1] for r in range(raw - 1)]
-        res = []
         for m in range(outs // 4):
             chosen = []
             for k in range(4):
@@ -214,55 +223,94 @@
             for k in range(4):
                 l = 4 * m + k
                 at = slice(k * ROWS, (k + 1) * ROWS)
-                base = (l + HALO - 2) * SLOT + ROWS
-                value = pad_ref[i, base : base + ROWS, :] - numer[at] / (denom[at] + outside)
+                base = (l + REACH) * SLOT + ROWS
+                value = tpad_ref[base : base + ROWS, :] - numer[at] / (denom[at] + outside)
                 if l < 2:
                     value = value * not_first
                 if l >= w + 2:
                     value = value * not_last
-                value = value.astype(BF16).astype(F32)
-                res.append(value)
-                res_ref[l * SLOT + ROWS : (l + 1) * SLOT, :] = value
-
-        def convolve(ref, count, weight):
-            first, second = [], []
-            for l in range(count):
-                base = l * SLOT + ROWS
-                first.append(jnp.where(low8, ref[base - 1 : base - 1 + ROWS, :], ref[base : base + ROWS, :]))
-                second.append(ref[base + 1 : base + 1 + ROWS, :])
-            rows = jnp.concatenate([jnp.concatenate(first, 0), jnp.concatenate(second, 0)], 1).astype(BF16)
-            full = jnp.dot(rows, weight, preferred_element_type=F32)
-            full = [full[l * ROWS : (l + 1) * ROWS] for l in range(count)]
-            return [
-                full[x][:, :LANES] + full[x + 1][:, LANES : 2 * LANES] + full[x + 2][:, 2 * LANES :]
-                for x in range(count - 2)
-            ]
-
-        for h, value in enumerate(convolve(res_ref, outs, weights[0])):
-            value = jnp.maximum(value, 0.0).astype(BF16).astype(F32)
-            if h == 0:
-                value = value * not_first
-            if h == w + 1:
-                value = value * not_last
-            hid_ref[h * SLOT + ROWS : (h + 1) * SLOT, :] = value
-        found = jnp.zeros((ROWS, LANES), F32)
-        for x, value in enumerate(convolve(hid_ref, w + 2, weights[1])):
-            refined = res[x + 2] + value
-            mean = jnp.sum(refined * refined, axis=1, keepdims=True) * (1.0 / LANES)
-            found = jnp.where(lane8 == x, mean, found)
-
-        out_ref[2 * i + core] = found
-        out_ref[2 * i + 1 - core] = jnp.zeros((ROWS, LANES), F32)
-        mask = jnp.where(lane8 < w, mask, 0.0)
-        total = jnp.sum(jnp.sum(found * mask, axis=1, keepdims=True), axis=0, keepdims=True)
-        count = jnp.sum(jnp.sum(mask, axis=1, keepdims=True), axis=0, keepdims=True)
-        here = sub8 == zone
-        zones = zones + jnp.where(here & (lane8 == w), total, 0.0)
-        return zones + jnp.where(here & (lane8 == w + 1), count, 0.0)
-
-    zones = lax.fori_loop(0, chips, one_die, jnp.zeros((ROWS, LANES), F32))
+                res_ref[i, l * SLOT + ROWS : (l + 1) * SLOT, :] = value.astype(BF16).astype(F32)
+
+    def align_step(step, carry):
+        for u in range(PAIR):
+            i = PAIR * step + u
+            for x in range(outs + 1):
+                res_ref[i, x * SLOT : x * SLOT + ROWS, :] = zero8
+            align(i, pick(golds, step, u), *scratch[7 * u : 7 * u + 7])
+        return carry
+
+    lax.fori_loop(0, chips // PAIR, align_step, 0)
+
+    def convolve(read, count, weight):
+        first, second = [], []
+        for l in range(count):
+            base = l * SLOT + ROWS
+            first.append(jnp.where(low8, read(base - 1), read(base)))
+            second.append(read(base + 1))
+        rows = jnp.concatenate([jnp.concatenate(first, 0), jnp.concatenate(second, 0)], 1).astype(BF16)
+        full = jnp.dot(rows, weight, preferred_element_type=F32)
+        full = [full[l * ROWS : (l + 1) * ROWS] for l in range(count)]
+        return [
+            full[x][:, :LANES] + full[x + 1][:, LANES : 2 * LANES] + full[x + 2][:, 2 * LANES :]
+            for x in range(count - 2)
+        ]
+
+    def hidden_step(step, carry):
+        for u in range(PAIR):
+            i = PAIR * step + u
+            for x in range(w + 3):
+                hid_ref[i, x * SLOT : x * SLOT + ROWS, :] = zero8
+            for h, value in enumerate(convolve(lambda at: res_ref[i, at : at + ROWS, :], outs, weights[0])):
+                value = jnp.maximum(value, 0.0).astype(BF16).astype(F32)
+                if h == 0:
+                    value = value * not_first
+                if h == w + 1:
+                    value = value * not_last
+                hid_ref[i, h * SLOT + ROWS : (h + 1) * SLOT, :] = value
+        return carry
+
+    lax.fori_loop(0, chips // PAIR, hidden_step, 0)
+
+    def energy_step(step, sums):
+        for u in range(PAIR):
+            i = PAIR * step + u
+            found = zero8
+            for x, value in enumerate(convolve(lambda at: hid_ref[i, at : at + ROWS, :], w + 2, weights[1])):
+                base = (x + 2) * SLOT + ROWS
+                refined = res_ref[i, base : base + ROWS, :] + value
+                mean = jnp.sum(refined * refined, axis=1, keepdims=True) * (1.0 / LANES)
+                found = jnp.where(lane8 == x, mean, found)
+            out_ref[2 * i + core] = found
+            out_ref[2 * i + 1 - core] = zero8
+            mask = own_ref[i, :, half // 2 * LANES :].astype(F32)[:ROWS]
+            mask = jnp.where(lane8 < w, mask, 0.0)
+            total = jnp.sum(jnp.sum(found * mask, axis=0, keepdims=True), axis=1, keepdims=True)
+            count = jnp.sum(jnp.sum(mask, axis=0, keepdims=True), axis=1, keepdims=True)
+            here = sub8 == pick(zones, step, u)
+            sums = sums + jnp.where(here & (lane8 == w), total, 0.0) + jnp.where(here & (lane8 == w + 1), count, 0.0)
+        return sums
+
+    sums = lax.fori_loop(0, chips // PAIR, energy_step, zero8)
     for d in range(2 * chips):
-        out_ref[d] = out_ref[d] + zones
+        out_ref[d] = out_ref[d] + sums
+
+
+def scratches(n, w):
+    cols, raw, outs = w + 2 * HALO, w + 4 + 2 * REACH, w + 4
+    lanes_g = -(-cols * SLOT // LANES) * LANES
+    one = [
+        pltpu.VMEM((cols * SLOT + ROWS, LANES), F32),
+        pltpu.VMEM((raw * SLOT + ROWS, LANES), F32),
+        pltpu.VMEM((raw * ROWS, 3 * LANES), BF16),
+        pltpu.VMEM((cols * SLOT, 3 * LANES), BF16),
+        pltpu.VMEM((cols * SLOT, LANES), BF16),
+        pltpu.VMEM((lanes_g, LANES), BF16),
+        pltpu.VMEM((outs * SLOT + ROWS, LANES), F32),
+    ]
+    return [
+        pltpu.VMEM((n // 2, outs * SLOT + ROWS, LANES), F32),
+        pltpu.VMEM((n // 2, (w + 2) * SLOT + ROWS, LANES), F32),
+    ] + one * PAIR
 
 
 def score_kernel(chips, w, zone_ref, back_ref, out_ref):
@@ -287,8 +335,6 @@
     chips = n // 2
     w = defect_mask.shape[2] // chips
     cols = w + 2 * HALO
-    raw = w + 4 + 2 * REACH
-    outs = w + 4
     half = cols // 2
     length = half * C + LANES
     smem = pl.BlockSpec(memory_space=pltpu.SMEM)
@@ -306,22 +352,12 @@
     own = lax.all_to_all(packed, "col", 0, 0, axis_index_groups=groups, tiled=True)
     other = lax.ppermute(own, "col", [(d, d ^ 1) for d in range(n)])
     me = lax.axis_index("col").astype(jnp.int32).reshape(1)
-    lanes_g = -(-cols * SLOT // LANES) * LANES
     partial = pl.pallas_call(
         functools.partial(main_kernel, chips, w),
         out_shape=jax.ShapeDtypeStruct((n, ROWS, LANES), F32),
         in_specs=[smem, smem, vmem, vmem, vmem],
         out_specs=vmem,
-        scratch_shapes=[
-            pltpu.VMEM((n, cols * SLOT + ROWS, LANES), F32),
-            pltpu.VMEM((raw * ROWS, 3 * LANES), BF16),
-            pltpu.VMEM((cols * SLOT, 3 * LANES), BF16),
-            pltpu.VMEM((cols * SLOT, LANES), BF16),
-            pltpu.VMEM((lanes_g, LANES), BF16),
-            pltpu.VMEM((outs * SLOT + ROWS, LANES), F32),
-            pltpu.VMEM((outs * SLOT + ROWS, LANES), F32),
-            pltpu.VMEM(((w + 2) * SLOT + ROWS, LANES), F32),
-        ],
+        scratch_shapes=scratches(n, w),
         compiler_params=params,
     )(me, golden_owner, own, other, kernels)
     back = lax.all_to_all(partial, "col", 0, 0, tiled=True)

time: 48 us -> 41.9 us (0.87)
  Pallas kernels: 15.9 us -> 9.84 us
    pallas_call x1, Pallas kernels: 15.2 us -> 9.05 us  [body(): pl.pallas_call(functools.partial(main_kernel, chips, w), out_shape=jax.Sh...]
where the time goes in v2:
time: 41.9 us; the launch traced here: 41.6 us
  blocking collectives  27.9 us (67%)
  Pallas kernels  9.84 us (23%)
  local copies, waits for them, and re-layouts  1.79 us (4%)
  waiting for transfers between devices  1.42 us (3%)
  between operations  0.68 us (2%)
    all_to_all x1, blocking collectives, body(): lax.all_to_all(packed, 'col', 0, 0, axis_index_groups=groups, tiled=True)  18.1 us
    all_to_all x1, blocking collectives, body(): back = lax.all_to_all(partial, 'col', 0, 0, tiled=True)  9.79 us
    pallas_call x1, Pallas kernels, body(): pl.pallas_call(functools.partial(main_kernel, chips, w), out_shape=jax.Sh...  9.05 us
    unnamed x9, local copies, waits for them, and re-layouts  1.79 us
    ppermute x1, waiting for transfers between devices, body(): other = lax.ppermute(own, 'col', [(d, d ^ 1) for d in range(n)])  1.42 us
  transfers between devices with their start and end apart: 1, of which 1 were waited for; matrix products, arithmetic and copies ran while one was open for 0% of the time, Pallas kernels for 0%

profile of v2, /device:TPU:0, one launch (start us, length us, event | category | flops | bytes accessed | tf_op | source)
XLA Modules:
  0.0 41.6 jit_solution(17092709884432005623)
XLA Ops:
  0.7 0.0 copy-start
  0.7 0.9 %copy-done = bf16[1,8,8192]{2,1,0:T(8,128)(2,1)S(1)} copy-done((bf16[1,8,8192]{2,1,0:T(8,128)(2,1)S(1)}, bf16[1,8,8192]{2,1,0:T(8,128)(2,1)}, u32[]{:S(2)}) %copy-start) | copy-done | bytes 131096
  1.6 0.0 copy-start.1
  1.6 0.7 %copy-done.1 = s32[1,8,128]{2,1,0:T(8,128)S(1)} copy-done((s32[1,8,128]{2,1,0:T(8,128)S(1)}, s32[1,8,128]{2,1,0:T(8,128)}, u32[]{:S(2)}) %copy-start.1) | copy-done | bytes 4120
  2.2 0.1 shard_map.55
  2.3 0.0 copy-start.3
  2.3 18.1 %all_to_all.10.own_ref = bf16[8,16,1280]{2,1,0:T(8,128)(2,1)S(1)} all-to-all(bf16[8,16,1280]{2,1,0:T(8,128)(2,1)S(1)} %shard_map.55), channel_id=1, replica_groups={{0,2,4,6,8,10,12,14},{1,3,5,7,9,11,13,15},{16,18,20,22,24,26,28,30},{17..., dimensions={0} | all-to-all | bytes 655360 | tf_op jit(solution)/shard_map/all_to_all | solution.py:352
  20.4 0.0 collective-permute-start
  20.5 0.0 copy-done.3
  20.5 0.2 copy.6.kern_ref
  20.6 0.0 copy-start.2
  20.7 1.4 %collective-permute-done.other_ref = bf16[8,16,1280]{2,1,0:T(8,128)(2,1)S(1)} collective-permute-done((bf16[8,16,1280]{2,1,0:T(8,128)(2,1)S(1)}, bf16[8,16,1280]{2,1,0:T(8,128)(2,1)S(1)}, u32[]{:S(2)}, u32[]{:S(2)}) %collective-permute-start) | collective-permute-done | bytes 327712 | tf_op jit(solution)/shard_map/ppermute | solution.py:353
  22.1 0.0 copy-done.2
  22.1 9.0 %shard_map.56 = f32[16,8,128]{2,1,0:T(8,128)S(1)} custom-call(s32[1]{0:T(128)} %bitcast.me_ref, s32[8]{0:T(128)S(1)} %copy-done.2, bf16[8,16,1280]{2,1,0:T(8,128)(2,1)S(1)} %all_to_all.10.own_ref, bf16[8,16,1280]{2,1,0:T(8,128)(2,1)S(1)} %collective-permute-done.other_ref, bf16[2,576,64]{2,1,0:T(8,128)(2,1)S(1)} %copy.6.kern_ref), custom_call_target="tpu_custom_call" | custom-call | tf_op jit(solution)/shard_map/pallas_call | solution.py:355
  31.1 9.8 %all_to_all.11.back_ref = f32[16,8,128]{2,1,0:T(8,128)S(1)} all-to-all(f32[16,8,128]{2,1,0:T(8,128)S(1)} %shard_map.56), channel_id=1, replica_groups=mesh['groups'=2,'col'=16] {'col'}, dimensions={0} | all-to-all | bytes 131072 | tf_op jit(solution)/shard_map/all_to_all | solution.py:363
  40.9 0.7 %shard_map.57 = f32[1,8,128]{2,1,0:T(8,128)} custom-call(s32[1]{0:T(128)S(6)} %copy.7.zone_ref, f32[16,8,128]{2,1,0:T(8,128)S(1)} %all_to_all.11.back_ref), custom_call_target="tpu_custom_call" | custom-call | tf_op jit(solution)/shard_map/pallas_call | solution.py:364
Async XLA Ops:
  0.7 0.9 %copy-start = (bf16[1,8,8192]{2,1,0:T(8,128)(2,1)S(1)}, bf16[1,8,8192]{2,1,0:T(8,128)(2,1)}, u32[]{:S(2)}) copy-start(bf16[1,8,8192]{2,1,0:T(8,128)(2,1)} %feat_ref.1) | copy-start | bytes 393220
  1.6 0.7 %copy-start.1 = (s32[1,8,128]{2,1,0:T(8,128)S(1)}, s32[1,8,128]{2,1,0:T(8,128)}, u32[]{:S(2)}) copy-start(s32[1,8,128]{2,1,0:T(8,128)} %mask_ref.1) | copy-start | bytes 12292
  2.3 18.1 %copy-start.3 = (bf16[2,576,64]{1,2,0:T(8,128)(2,1)S(1)}, bf16[2,576,64]{1,2,0:T(8,128)(2,1)}, u32[]{:S(2)}) copy-start(bf16[2,576,64]{1,2,0:T(8,128)(2,1)} %param.9) | copy-start | bytes 442372
  20.4 1.6 %collective-permute-start = (bf16[8,16,1280]{2,1,0:T(8,128)(2,1)S(1)}, bf16[8,16,1280]{2,1,0:T(8,128)(2,1)S(1)}, u32[]{:S(2)}, u32[]{:S(2)}) collective-permute-start(bf16[8,16,1280]{2,1,0:T(8,128)(2,1)S(1)} %all_to_all.10.own_ref), channel_id=1, source_target_pairs={{0,1},{1,0},{2,3},{3,2},{4,5},{5,4},{6,7},{7,6},{8,9},{9,8},{10,11... | collective-permute-start | bytes 983048 | tf_op jit(solution)/shard_map/ppermute | solution.py:353
  20.6 1.4 %copy-start.2 = (s32[8]{0:T(128)S(1)}, s32[8]{0:T(128)}, u32[]{:S(2)}) copy-start(s32[8]{0:T(128)} %owner_ref.1) | copy-start | bytes 100

commit v3 on v0

v3 whole, which is shorter than its diff:
```python
import functools

import jax
import jax.numpy as jnp
from jax import lax
from jax.experimental import pallas as pl
from jax.experimental.pallas import tpu as pltpu
from jax.sharding import PartitionSpec as P

C = 64
SHIFT = 6
BOX = 5
Z = 8
SIDE = 2 * SHIFT + 1
REACH = BOX // 2
HALO = SHIFT + REACH + 2
ROWS = 8
SLOT = 16
TOP = (SLOT - ROWS) // 2
LANES = 128
GROUP = 4
FACTOR = 32.0 * 1.4426950408889634
F32 = jnp.float32
BF16 = jnp.bfloat16


def iota(shape, dim):
    return lax.broadcasted_iota(jnp.int32, shape, dim)


def pack_kernel(chips, w, feat_ref, tail_ref, out_ref):
    half = (w + 2 * HALO) // 2
    width = tail_ref.shape[1]
    mask = tail_ref[:ROWS].astype(F32)
    zone = tail_ref[ROWS:].astype(F32)
    lane = iota((ROWS, LANES), 1)
    for p in range(chips):
        for t in range(half // 2):
            parts = []
            for part in range(2):
                col = p * w - HALO + part * half + 2 * t
                if 0 <= col < width:
                    parts.append(feat_ref[0, :, col * C : (col + 2) * C].astype(F32))
                else:
                    parts.append(jnp.zeros((ROWS, LANES), F32))
            out_ref[p, :, t * LANES : (t + 1) * LANES] = jnp.concatenate(parts, 0).astype(BF16)
        here = pltpu.roll(mask, (width - p * w) % width, 1) if p else mask
        here = jnp.where(lane < w, here, 0.0)
        last = jnp.concatenate([here, zone], 0)
        out_ref[p, :, half // 2 * LANES :] = last.astype(BF16)


def split_square(values):
    square = values * values
    high = square.astype(BF16).astype(F32)
    return high, square - high


def place(values):
    row, col = iota((LANES, LANES), 0), iota((LANES, LANES), 1)
    highs, lows = zip(*(split_square(value) for value in values))
    squares = [jnp.concatenate([part.astype(BF16) for part in parts], 1) for parts in (highs, lows)]
    picks = [(col == 2 * q + row // C).astype(BF16) for q in range(len(values))]
    sums = jnp.dot(jnp.concatenate(squares, 0), jnp.concatenate(picks, 0), preferred_element_type=F32)
    rows = sums.shape[0] // 2
    return sums[:rows] + sums[rows:]


def test_kernel(chips, w, own_ref, test_ref, box_ref, wide_ref, *scratch):
    half = (w + 2 * HALO) // 2
    raw = w + 4 + 2 * REACH
    before = HALO - REACH - 2
    zero8 = jnp.zeros((ROWS, LANES), F32)
    lo, hi = slice(0, C), slice(C, LANES)

    for ref in scratch:
        for i in range(0, ref.shape[0], ROWS):
            ref[i : i + ROWS, :] = zero8
    pairs = []
    for part in range(2):
        for t in range(half // 2):
            if 0 <= part * half + 2 * t - before < raw:
                rows = slice(part * ROWS, (part + 1) * ROWS)
                pairs.append([own_ref[i, :, t * LANES : (t + 1) * LANES].astype(F32)[rows] for i in range(chips)])
    parts = [split_square(jnp.concatenate([tiles[i] for tiles in pairs], 0)) for i in range(chips)]
    squares = [jnp.concatenate([part[k].astype(BF16) for part in parts], 0) for k in range(2)]
    both = (iota((2 * LANES, 2 * LANES), 0) % LANES // C == iota((2 * LANES, 2 * LANES), 1) // LANES).astype(BF16)
    wide_ref[...] = jnp.dot(jnp.concatenate(squares, 1), both, preferred_element_type=F32)
    scale = 1.0 / FACTOR**2
    for i in range(chips):
        energy = []
        for r in range(raw):
            row = (i * (raw // 2) + r // 2) * ROWS
            energy.append(wide_ref[row : row + ROWS, r % 2 * LANES : (r % 2 + 1) * LANES])
        twos = [x + y for x, y in zip(energy, energy[1:])]
        ref = scratch[6 + i % 2]
        for l in range(w + 4):
            ref[l * SLOT + ROWS : (l + 1) * SLOT, :] = (twos[l] + twos[l + 2] + energy[l + 4]) * scale
        for l in range(w + 4):
            base = l * SLOT + ROWS
            rows = [ref[base + dy : base + dy + ROWS, :] for dy in range(-2, 3)]
            box_ref[i, l * ROWS : (l + 1) * ROWS, :] = sum(rows[1:], rows[0])

    for i in range(chips):
        refs = scratch[3 * (i % 2) : 3 * (i % 2) + 3]
        for q in range(raw // 2):
            here = pairs[q][i]
            turned = pltpu.roll(here, C, 1)
            for odd, (left, right) in enumerate(((here, turned), (turned, here))):
                top = (2 * q + odd) * SLOT + ROWS
                refs[0][top + 2 : top + 2 + ROWS, lo] = left[:, lo]
                refs[0][top + 1 : top + 1 + ROWS, hi] = right[:, hi]
                refs[1][top : top + ROWS, lo] = left[:, lo]
                refs[2][top - 1 : top - 1 + ROWS, lo] = left[:, lo]
                refs[2][top - 2 : top - 2 + ROWS, hi] = right[:, hi]
        for r in range(0, raw, 2):
            at = slice(r * ROWS, (r + 2) * ROWS)
            for t, ref in enumerate(refs):
                two = [ref[q * SLOT + ROWS : (q + 1) * SLOT, :] for q in (r, r + 1)]
                test_ref[i, at, t * LANES : (t + 1) * LANES] = jnp.concatenate(two, 0).astype(BF16)
            test_ref[i, at, 3 * LANES :] = jnp.zeros((2 * ROWS, LANES), BF16)


def main_kernel(
    chips, w, me_ref, owner_ref, own_ref, other_ref, test_ref, box_ref, kern_ref, out_ref,
    res_ref, hid_ref, g0_ref, g1_ref, g2_ref, gsq_ref, weight_ref, *scratch
):
    cols = w + 2 * HALO
    half = cols // 2
    raw = w + 4 + 2 * REACH
    outs = w + 4
    odds = half * SLOT
    chunks = -(-half // 8)
    lanes_g = chunks * LANES
    golds_ref = scratch[:4]
    kept = [scratch[4 + k * (chunks + 1) : 4 + (k + 1) * (chunks + 1)] for k in range(3)]
    me = me_ref[0]
    chip = me // 2
    core = me % 2
    not_first = jnp.where(chip == 0, 0.0, 1.0).astype(F32)
    not_last = jnp.where(chip == chips - 1, 0.0, 1.0).astype(F32)

    lane8 = iota((ROWS, LANES), 1)
    sub8 = iota((ROWS, LANES), 0)
    low8 = lane8 < C
    zero8 = jnp.zeros((ROWS, LANES), F32)
    lo = slice(0, C)
    hi = slice(C, LANES)

    twice = (iota((C, LANES), 1) % C == iota((C, LANES), 0)).astype(BF16)
    low = iota((C, LANES), 1) < C
    for conv in range(2):
        doubled = lax.dot_general(kern_ref[conv], twice, (((0,), (0,)), ((), ())), preferred_element_type=F32)
        for dy in range(3):
            for at in range(4):
                taps = [
                    doubled[(3 * dy + dx) * C : (3 * dy + dx + 1) * C] if 0 <= dx < 3 else jnp.zeros((C, LANES), F32)
                    for dx in (at, at - 1)
                ]
                row = (4 * dy + at) * C
                weight_ref[conv, row : row + C, :] = jnp.where(low, taps[0], taps[1]).astype(BF16)

    zones = [
        [ref[i, :, half // 2 * LANES :].astype(F32)[ROWS, 0].astype(jnp.int32) for i in range(chips)]
        for ref in (own_ref, other_ref)
    ]
    golds = [owner_ref[zone] for zone in zones[0]]

    for ref in (g0_ref, g1_ref, g2_ref, gsq_ref):
        for i in range(0, ref.shape[0], ROWS):
            ref[i : i + ROWS, :] = jnp.where(low8, 0.0, 1.0) if ref is g1_ref else zero8
    summing = (iota((SLOT, 4 * LANES), 1) >= 3 * LANES).astype(BF16)

    valid = []
    for k in range(4):
        a = lane8 % SLOT - TOP - sub8
        both = []
        for parity in range(2):
            b = lane8 // SLOT * 2 + parity - k
            both.append((b >= 0) & (b < SIDE) & (jnp.abs(a) <= SHIFT))
        valid.append(both)
    outside = jnp.maximum(SHIFT - TOP - sub8, 0) + jnp.maximum(sub8 + SHIFT - (SLOT - TOP - 1), 0)
    outside = (outside * SIDE).astype(F32)

    def stage(i, gold_ref):
        owner = golds[i]
        mine = owner % 2 == core
        for t in range(half // 2):
            at = slice(t * LANES, (t + 1) * LANES)
            tile = jnp.where(mine, own_ref[owner // 2, :, at], other_ref[owner // 2, :, at]).astype(F32)
            for part in range(2):
                here = tile[part * ROWS : (part + 1) * ROWS]
                turned = pltpu.roll(here, C, 1)
                for odd, (left, right) in enumerate(((here, turned), (turned, here))):
                    top = odd * odds + (part * half // 2 + t) * SLOT + TOP
                    g0_ref[top + 2 : top + 2 + ROWS, lo] = left[:, lo]
                    g0_ref[top + 1 : top + 1 + ROWS, hi] = right[:, hi]
                    g1_ref[top : top + ROWS, lo] = left[:, lo]
                    g2_ref[top - 1 : top - 1 + ROWS, lo] = left[:, lo]
                    g2_ref[top - 2 : top - 2 + ROWS, hi] = right[:, hi]
                    high, low = split_square(jnp.where(low8, left, right))
                    gsq_ref[top : top + ROWS, :] = jnp.where(low8, high, low)
            yield
        for parity in range(2):
            for g in range(half):
                at = slice(parity * odds + g * SLOT, parity * odds + (g + 1) * SLOT)
                for t, ref in enumerate((g0_ref, g1_ref, g2_ref, gsq_ref)):
                    gold_ref[at, t * LANES : (t + 1) * LANES] = ref[at, :].astype(BF16)
                if g % 6 == 5:
                    yield

    def right(value, slots):
        return pltpu.roll(value, slots * SLOT, 1) if slots else value

    def windows(gold_ref, tile, at):
        rows = [slice(p * odds + tile * SLOT, p * odds + (tile + 8) * SLOT) for p in range(2)]
        return jnp.concatenate([gold_ref[rows[0], at], gold_ref[rows[1], at]], 0)

    def first_pair(v):
        return max(0, 8 * v - SHIFT)

    def products(i, kept, gold_ref):
        energies = ([], [])
        for v in range(chunks):
            first, last = first_pair(v), min(raw // 2 - 1, 8 * v + 7)
            tiles = min(8, half - 8 * v)
            rows = [slice(p * odds + 8 * v * SLOT, p * odds + (8 * v + (tiles if tiles <= 4 else 8)) * SLOT) for p in range(2)]
            parts = [gold_ref[rows[0], :], gold_ref[rows[1], :]]
            if tiles < 4:
                parts.append(gold_ref[: (8 - 2 * tiles) * SLOT, :])
            block = lax.dot_general(
                jnp.concatenate([summing, test_ref[i, 2 * first * ROWS : 2 * (last + 1) * ROWS, :]], 0),
                jnp.concatenate(parts, 0),
                (((1,), (1,)), ((), ())),
                preferred_element_type=F32,
            )
            for p in range(2):
                at = slice(p * LANES, (p + 1) * LANES) if tiles > 4 else slice(0, LANES)
                start = 0 if tiles > 4 else p * tiles * SLOT
                here = block[:ROWS, at]
                energies[p].append(pltpu.roll(here, LANES - start, 1) if start else here)
            kept[v][...] = block[SLOT:]
            yield

        by_parity = []
        for parity in range(2):
            parts = []
            for here in energies[parity]:
                down = here
                for dy in (-2, -1, 1, 2):
                    inside = (sub8 + dy >= 0) & (sub8 + dy < ROWS)
                    down = down + jnp.where(inside, pltpu.roll(here, (-dy) % LANES, 1), 0.0)
                parts.append(down)
            by_parity.append(jnp.concatenate(parts, 1))
        even, odd = by_parity
        even1, even2 = (pltpu.roll(even, lanes_g - d * SLOT, 1) for d in (1, 2))
        odd1, odd2 = (pltpu.roll(odd, lanes_g - d * SLOT, 1) for d in (1, 2))
        def window(values, m):
            v, offset = divmod(2 * m * SLOT, LANES)
            first = values[:, v * LANES : (v + 1) * LANES]
            if not offset:
                return first
            second = values[:, (v + 1) * LANES : (v + 2) * LANES]
            return pltpu.roll(jnp.where(lane8 >= offset, first, second), LANES - offset, 1)

        for p, terms in enumerate(((even, odd, even1, odd1, even2), (odd, even1, odd1, even2, odd2))):
            a, b, c, d, e = terms
            rows = [(m, a + b + c + d + e) for m in range(outs // 4)]
            rows.append((0, c + d + e + not_first * (a + b)))
            rows.append((0, b + c + d + e + not_first * a))
            rows.append((w // 4, a + b + c + d + not_last * e))
            rows.append((w // 4, a + b + c + not_last * (d + e)))
            for row, (m, values) in enumerate(rows):
                kept[chunks][row * ROWS : (row + 1) * ROWS, p * LANES : (p + 1) * LANES] = window(values, m)
            yield

    def average(i, kept, gold_ref):
        special = {l: outs // 4 + k for k, l in enumerate((2, 3, w, w + 1))}

        def piece(r, parity, v):
            row = (r - 2 * first_pair(v)) * ROWS
            tiles = half - 8 * v
            if tiles > 4:
                return kept[v][row : row + ROWS, parity * LANES : (parity + 1) * LANES], 0
            return kept[v][row : row + ROWS, :], parity * tiles * SLOT

        def shear(r, parity, more):
            v, slots = divmod(r // 2 + more, 8)
            value, start = piece(r, parity, v)
            if slots + SHIFT - more >= 8:
                value2, start2 = piece(r, parity, v + 1)
                if start2:
                    value2 = pltpu.roll(value2, LANES - start2, 1)
                value = jnp.where(lane8 >= slots * SLOT, value, value2)
            turn = start + slots * SLOT
            return pltpu.roll(value, LANES - turn, 1) if turn else value

        def finish(m, weight):
            values = windows(gold_ref, 2 * m + 1, slice(LANES, 2 * LANES))
            total = jnp.dot(weight, values, preferred_element_type=F32)
            for k in (0, 2):
                pair = (4 * m + k) // 2
                even, odd = total[k * ROWS : (k + 1) * ROWS], total[(k + 1) * ROWS : (k + 2) * ROWS]
                numer = jnp.where(low8, even, pltpu.roll(odd, C, 1))
                denom = jnp.where(low8, pltpu.roll(even, C, 1), odd) + outside
                part, t = divmod(HALO // 2 - 1 + pair, half // 2)
                test = own_ref[i, :, t * LANES : (t + 1) * LANES].astype(F32)[part * ROWS : (part + 1) * ROWS]
                value = test - numer / denom
                if pair == 0:
                    value = value * not_first
                if pair == outs // 2 - 1:
                    value = value * not_last
                res_ref[i, pair * SLOT + ROWS : (pair + 1) * SLOT, :] = value.astype(BF16).astype(F32)

        sheared, pairs = [], []

        def extend(count):
            for r in range(len(sheared), count):
                odd = r % 2
                sheared.append((shear(r, odd, 0), shear(r, 1 - odd, odd)))
                if r:
                    pairs.append(tuple(x + y for x, y in zip(sheared[r - 1], sheared[r])))

        for m in range(outs // 4):
            extend(4 * m + 8)
            chosen = []
            for k in range(4):
                l = 4 * m + k
                cross = [pairs[l][b] + pairs[l + 2][b] + sheared[l + 4][b] for b in range(2)]
                cross = [right(cross[k % 2], (k + 1) // 2 if k % 2 else k // 2), right(cross[1 - k % 2], k // 2)]
                mine = box_ref[i, l * ROWS : (l + 1) * ROWS, :]
                row = special.get(l, m) * ROWS
                both = []
                for p in range(2):
                    other = kept[chunks][row : row + ROWS, p * LANES : (p + 1) * LANES]
                    scale = lax.rsqrt(mine * other + 1e-05 / FACTOR**2)
                    both.append(jnp.where(valid[k][p], jnp.exp2(cross[p] * scale), 0.0))
                chosen.append(jnp.concatenate(both, 1))
            weight = jnp.concatenate(chosen, 0).astype(BF16)
            if m:
                finish(m - 1, before)
            before = weight
            yield
        finish(outs // 4 - 1, before)
        yield

    for i in range(chips):
        for x in range(outs // 2 + 1):
            res_ref[i, x * SLOT : x * SLOT + ROWS, :] = zero8
        for x in range(w // 2 + 2):
            hid_ref[i, x * SLOT : x * SLOT + ROWS, :] = zero8
    def convolve(ref, count, weight, dies):
        tiles = []
        for dy in (-1, 0, 1):
            for which in range(2):
                rows = [
                    ref[i, (p + which) * SLOT + ROWS + dy : (p + which + 1) * SLOT + dy, :]
                    for i in dies
                    for p in range(count)
                ]
                tiles.append(jnp.concatenate(rows, 0).astype(BF16))
        full = jnp.dot(jnp.concatenate(tiles, 1), weight, preferred_element_type=F32)
        return [
            (i, [full[(k * count + p) * ROWS : (k * count + p + 1) * ROWS] for p in range(count)])
            for k, i in enumerate(dies)
        ]

    def finish_dies(dies):
        for i, values in convolve(res_ref, outs // 2 - 1, weight_ref[0], dies):
            for p, value in enumerate(values):
                value = jnp.maximum(value, 0.0).astype(BF16).astype(F32)
                if p == 0:
                    value = jnp.where(low8, value * not_first, value)
                if p == w // 2:
                    value = jnp.where(low8, value, value * not_last)
                hid_ref[i, p * SLOT + ROWS : (p + 1) * SLOT, :] = value
        yield
        for i, values in convolve(hid_ref, w // 2, weight_ref[1], dies):
            for p, value in enumerate(values):
                refined[p].append(res_ref[i, (p + 1) * SLOT + ROWS : (p + 2) * SLOT, :] + value)
        yield

    refined = [[] for p in range(w // 2)]
    for slot in range(chips + 4):
        running = []
        if 0 <= slot - 1 < chips:
            i = slot - 1
            running.append(products(i, kept[i % 3], golds_ref[i % 4]))
        if 0 <= slot - 3 < chips:
            i = slot - 3
            running.append(average(i, kept[i % 3], golds_ref[i % 4]))
        if slot < chips:
            running.append(stage(slot, golds_ref[slot % 4]))
        for k in range(0, chips, GROUP):
            if slot == k + GROUP - 1 + 4:
                running.append(finish_dies(range(k, k + GROUP)))
        while running:
            running = [work for work in running if next(work, running) is not running]

    energy = place([jnp.concatenate(values, 0) for values in refined]) * (1.0 / C)
    sums = zero8
    for i in range(chips):
        found = energy[i * ROWS : (i + 1) * ROWS]
        out_ref[2 * i + core] = found
        mask = own_ref[i, :, half // 2 * LANES :].astype(F32)[:ROWS]
        mask = jnp.where(lane8 < w, mask, 0.0)
        total = jnp.sum(jnp.sum(found * mask, axis=0, keepdims=True), axis=1, keepdims=True)
        count = jnp.sum(jnp.sum(mask, axis=0, keepdims=True), axis=1, keepdims=True)
        both = jnp.where(lane8 == w, total, 0.0) + jnp.where(lane8 == w + 1, count, 0.0)
        sums = sums + jnp.where(sub8 == zones[0][i], both, 0.0)
    for i in range(chips):
        for which in range(2):
            mine = jnp.sum(jnp.where(sub8 == zones[which][i], sums, 0.0), axis=0, keepdims=True)
            mine = jnp.broadcast_to(mine, (ROWS, LANES))
            if which:
                out_ref[2 * i + 1 - core] = mine
            else:
                out_ref[2 * i + core] = out_ref[2 * i + core] + mine


def score_kernel(chips, w, back_ref, out_ref):
    lane = iota((ROWS, LANES), 1)
    total = back_ref[0]
    for d in range(1, 2 * chips):
        total = total + back_ref[d]
    zone_mean = total[:, w : w + 1] / jnp.maximum(total[:, w + 1 : w + 2], 1.0)
    energy = jnp.zeros((ROWS, LANES), F32)
    for p in range(chips):
        strip = back_ref[2 * p] + back_ref[2 * p + 1]
        strip = pltpu.roll(strip, p * w, 1) if p else strip
        energy = jnp.where((lane >= p * w) & (lane < (p + 1) * w), strip, energy)
    out_ref[0] = energy / (zone_mean + 0.01)


def body(n, features, zone_ids, golden_owner, defect_mask, kernels):
    chips = n // 2
    w = defect_mask.shape[2] // chips
    cols = w + 2 * HALO
    half = cols // 2
    raw = w + 4 + 2 * REACH
    length = half * C + LANES
    smem = pl.BlockSpec(memory_space=pltpu.SMEM)
    vmem = pl.BlockSpec(memory_space=pltpu.VMEM)
    params = pltpu.CompilerParams(vmem_limit_bytes=24 * 2**20)

    zone = jnp.pad(zone_ids.reshape(1, 1), ((0, ROWS - 1), (0, defect_mask.shape[2] - 1)))
    tail = jnp.concatenate([defect_mask[0], zone], 0)
    packed = pl.pallas_call(
        functools.partial(pack_kernel, chips, w),
        out_shape=jax.ShapeDtypeStruct((chips, 2 * ROWS, length), BF16),
        in_specs=[vmem] * 2,
        out_specs=vmem,
        compiler_params=params,
    )(features, tail)
    groups = [[2 * p + c for p in range(chips)] for c in range(2)]
    own = lax.all_to_all(packed, "col", 0, 0, axis_index_groups=groups, tiled=True)
    other = lax.ppermute(own, "col", [(d, d ^ 1) for d in range(n)])
    tests = pl.pallas_call(
        functools.partial(test_kernel, chips, w),
        out_shape=[
            jax.ShapeDtypeStruct((chips, raw * ROWS, 4 * LANES), BF16),
            jax.ShapeDtypeStruct((chips, (w + 4) * ROWS, LANES), F32),
        ],
        in_specs=[vmem],
        out_specs=[vmem] * 2,
        scratch_shapes=[
            pltpu.VMEM((chips * (raw // 2) * ROWS, 2 * LANES), F32),
        ]
        + [pltpu.VMEM((raw * SLOT + ROWS, LANES), F32)] * 6
        + [pltpu.VMEM(((w + 4) * SLOT + ROWS, LANES), F32)] * 2,
        compiler_params=params,
        cost_estimate=pl.CostEstimate(flops=10**9, bytes_accessed=10**6, transcendentals=0),
    )(own)
    me = lax.axis_index("col").astype(jnp.int32).reshape(1)
    chunks = -(-half // 8)
    reach = [min(raw // 2, 8 * v + 8) - max(0, 8 * v - SHIFT) for v in range(chunks)]
    kept = [
        pltpu.VMEM((2 * reach[v] * ROWS, (2 if half - 8 * v > 4 else 1) * LANES), F32) for v in range(chunks)
    ] + [pltpu.VMEM(((w // 4 + 5) * ROWS, 2 * LANES), F32)]
    rows = half * SLOT + -(-half // 8) * LANES
    partial = pl.pallas_call(
        functools.partial(main_kernel, chips, w),
        out_shape=jax.ShapeDtypeStruct((n, ROWS, LANES), F32),
        in_specs=[smem, smem] + [vmem] * 5,
        out_specs=vmem,
        scratch_shapes=[
            pltpu.VMEM((chips, (w // 2 + 2) * SLOT + ROWS, LANES), F32),
            pltpu.VMEM((chips, (w // 2 + 1) * SLOT + ROWS, LANES), F32),
        ]
        + [pltpu.VMEM((cols * SLOT, LANES), F32)] * 4
        + [pltpu.VMEM((2, 12 * C, LANES), BF16)]
        + [pltpu.VMEM((rows, 4 * LANES), BF16)] * 4
        + kept * 3,
        compiler_params=params,
    )(me, golden_owner, own, other, *tests, jnp.swapaxes(kernels, 1, 2))
    back = lax.all_to_all(partial, "col", 0, 0, tiled=True)
    return pl.pallas_call(
        functools.partial(score_kernel, chips, w),
        out_shape=jax.ShapeDtypeStruct(defect_mask.shape, F32),
        in_specs=[vmem],
        out_specs=vmem,
        compiler_params=params,
    )(back)


def solution(mesh):
    split = P(("groups", "col"), None, None)
    return jax.shard_map(
        functools.partial(body, mesh.shape["col"]),
        mesh=mesh,
        in_specs=(split, P(("groups", "col")), P("groups"), split, P()),
        out_specs=split,
        check_vma=False,
    )
```

time: 425 us -> 38.7 us (0.09)
  local copies, waits for them, and re-layouts: 179 us -> 0.91 us
  other arithmetic: 125 us -> 0.69 us
  waiting for transfers between devices: 43 us -> 0.69 us
  loops' own time: 27.6 us -> 0 us
  between operations: 15 us -> 0.67 us
  Pallas kernels: 0 us -> 7.68 us
    reshape x342 -> x0, local copies, waits for them, and re-layouts: 133 us -> none  [the longest x170 73.2 us: channel_sum(): return jnp.sum(values.reshape(values.shape[0], -1, chans), axis=-1)]
    add x197 -> x0, other arithmetic: 51.4 us -> none  [the longest x13 32.5 us: row_step(): numer = numer + jnp.repeat(expo, chans, axis=1) * moved]
    all_gather x1 -> x0, waiting for transfers between devices: 42.3 us -> none  [body(): piece = lax.all_gather(features, 'col', axis=0, tiled=True)]
    reduce_sum x175 -> x0, other arithmetic: 39.7 us -> none  [the longest x171 35.9 us: channel_sum(): return jnp.sum(values.reshape(values.shape[0], -1, chans), axis=-1)]
    broadcast_in_dim x170 -> x0, local copies, waits for them, and re-layouts: 32.5 us -> none  [the longest x169 32.3 us: row_step(): numer = numer + jnp.repeat(expo, chans, axis=1) * moved]
    psum x1 -> x0, blocking collectives: 31.4 us -> none  [body(): lax.psum((onehot * die_sum, onehot * die_count), 'col')]
    all_to_all x0 -> x2, blocking collectives: none -> 27.8 us  [the longest x1 18 us: body(): lax.all_to_all(packed, 'col', 0, 0, axis_index_groups=groups, tiled=True)]
    another operation x1 -> x0, loops' own time: 27.6 us -> none  [align_golden(): lax.scan(row_step, start, jnp.arange(side, dtype=jnp.int32))]
  transfers between devices with their start and end apart: 1 -> 1, of which waited for: 1 -> 1; matrix products, arithmetic and copies ran while one was open for 1% -> 0% of each run, Pallas kernels for 0% -> 2%
where the time goes in v3:
time: 38.7 us; the launch traced here: 38.4 us
  blocking collectives  27.8 us (72%)
  Pallas kernels  7.68 us (20%)
  local copies, waits for them, and re-layouts  0.91 us (2%)
  other arithmetic  0.69 us (2%)
  waiting for transfers between devices  0.69 us (2%)
  between operations  0.67 us (2%)
    all_to_all x1, blocking collectives, body(): lax.all_to_all(packed, 'col', 0, 0, axis_index_groups=groups, tiled=True)  18 us
    all_to_all x1, blocking collectives, body(): back = lax.all_to_all(partial, 'col', 0, 0, tiled=True)  9.8 us
    pallas_call x1, Pallas kernels, body(): pl.pallas_call(functools.partial(main_kernel, chips, w), out_shape=jax.Sh...  5.89 us
    pallas_call x1, Pallas kernels, body(): pl.pallas_call(functools.partial(test_kernel, chips, w), out_shape=[jax.S...  0.93 us
    unnamed x6, local copies, waits for them, and re-layouts  0.91 us
  transfers between devices with their start and end apart: 1, of which 1 were waited for; matrix products, arithmetic and copies ran while one was open for 0% of the time, Pallas kernels for 2%

profile of v3, /device:TPU:0, one launch (start us, length us, event | category | flops | bytes accessed | tf_op | source)
XLA Modules:
  0.0 38.4 jit_solution(2090877488913716481)
XLA Ops:
  0.7 0.7 %pad_add_fusion.tail_ref = s32[16,128]{1,0:T(8,128)S(1)} fusion(s32[1,1]{1,0:T(1,128)} %bitcast.4, s32[8,128]{1,0:T(8,128)} %bitcast.6), kind=kLoop, calls=%fused_computation | loop fusion | flops 2048 | bytes 12292 | tf_op jit(solution)/shard_map/concatenate | solution.py:447
  1.3 0.0 copy-start.1
  1.3 0.9 %copy-done.1 = bf16[1,8,8192]{2,1,0:T(8,128)(2,1)S(1)} copy-done((bf16[1,8,8192]{2,1,0:T(8,128)(2,1)S(1)}, bf16[1,8,8192]{2,1,0:T(8,128)(2,1)}, u32[]{:S(2)}) %copy-start.1) | copy-done | bytes 131096
  2.3 0.1 shard_map.55
  2.4 18.0 %all_to_all.10.own_ref = bf16[8,16,1280]{2,1,0:T(8,128)(2,1)S(1)} all-to-all(bf16[8,16,1280]{2,1,0:T(8,128)(2,1)S(1)} %shard_map.55), channel_id=1, replica_groups={{0,2,4,6,8,10,12,14},{1,3,5,7,9,11,13,15},{16,18,20,22,24,26,28,30},{17..., dimensions={0} | all-to-all | bytes 655360 | tf_op jit(solution)/shard_map/all_to_all | solution.py:456
  20.3 0.0 collective-permute-start
  20.3 0.0 copy-start
  20.3 0.0 copy-start.2
  20.3 0.9 %shard_map.56 = (bf16[8,192,512]{2,1,0:T(8,128)(2,1)S(1)}, f32[8,160,128]{2,1,0:T(8,128)S(1)}) custom-call(bf16[8,16,1280]{2,1,0:T(8,128)(2,1)S(1)} %all_to_all.10.own_ref), custom_call_target="tpu_custom_call" | custom-call | flops 1000000000 | bytes 1000000 | tf_op jit(solution)/shard_map/pallas_call | solution.py:458
  21.3 0.7 %collective-permute-done.other_ref = bf16[8,16,1280]{2,1,0:T(8,128)(2,1)S(1)} collective-permute-done((bf16[8,16,1280]{2,1,0:T(8,128)(2,1)S(1)}, bf16[8,16,1280]{2,1,0:T(8,128)(2,1)S(1)}, u32[]{:S(2)}, u32[]{:S(2)}) %collective-permute-start) | collective-permute-done | bytes 327712 | tf_op jit(solution)/shard_map/ppermute | solution.py:457
  22.0 0.0 copy-done
  22.0 0.0 copy-done.2
  22.0 5.9 %shard_map.57 = f32[16,8,128]{2,1,0:T(8,128)S(1)} custom-call(s32[1]{0:T(128)} %bitcast.me_ref, s32[8]{0:T(128)S(1)} %copy-done.2, bf16[8,16,1280]{2,1,0:T(8,128)(2,1)S(1)} %all_to_all.10.own_ref, bf16[8,16,1280]{2,1,0:T(8,128)(2,1)S(1)} %collective-permute-done.other_ref, bf16[8,192,512]{2,1,0:T(8,128)(2,1)S(1)} %get-tuple-element.7.test_ref, ...), custom_call_target="tpu_custom_call" | custom-call | tf_op jit(solution)/shard_map/pallas_call | solution.py:481
  27.9 9.8 %all_to_all.11.back_ref = f32[16,8,128]{2,1,0:T(8,128)S(1)} all-to-all(f32[16,8,128]{2,1,0:T(8,128)S(1)} %shard_map.57), channel_id=1, replica_groups=mesh['groups'=2,'col'=16] {'col'}, dimensions={0} | all-to-all | bytes 131072 | tf_op jit(solution)/shard_map/all_to_all | solution.py:496
  37.7 0.8 %shard_map.58 = f32[1,8,128]{2,1,0:T(8,128)} custom-call(f32[16,8,128]{2,1,0:T(8,128)S(1)} %all_to_all.11.back_ref), custom_call_target="tpu_custom_call" | custom-call | tf_op jit(solution)/shard_map/pallas_call | solution.py:497
Async XLA Ops:
  1.3 0.9 %copy-start.1 = (bf16[1,8,8192]{2,1,0:T(8,128)(2,1)S(1)}, bf16[1,8,8192]{2,1,0:T(8,128)(2,1)}, u32[]{:S(2)}) copy-start(bf16[1,8,8192]{2,1,0:T(8,128)(2,1)} %feat_ref.1) | copy-start | bytes 393220
  20.3 1.6 %collective-permute-start = (bf16[8,16,1280]{2,1,0:T(8,128)(2,1)S(1)}, bf16[8,16,1280]{2,1,0:T(8,128)(2,1)S(1)}, u32[]{:S(2)}, u32[]{:S(2)}) collective-permute-start(bf16[8,16,1280]{2,1,0:T(8,128)(2,1)S(1)} %all_to_all.10.own_ref), channel_id=1, source_target_pairs={{0,1},{1,0},{2,3},{3,2},{4,5},{5,4},{6,7},{7,6},{8,9},{9,8},{10,11... | collective-permute-start | bytes 983048 | tf_op jit(solution)/shard_map/ppermute | solution.py:457
  20.3 1.6 %copy-start = (bf16[2,576,64]{1,2,0:T(8,128)(2,1)S(1)}, bf16[2,576,64]{1,2,0:T(8,128)(2,1)}, u32[]{:S(2)}) copy-start(bf16[2,576,64]{1,2,0:T(8,128)(2,1)} %param.9) | copy-start | bytes 442372
  20.3 1.6 %copy-start.2 = (s32[8]{0:T(128)S(1)}, s32[8]{0:T(128)}, u32[]{:S(2)}) copy-start(s32[8]{0:T(128)} %owner_ref.1) | copy-start | bytes 100

commit v4 on v3

--- a/solution.py
+++ b/solution.py
@@ -18,7 +18,6 @@
 SLOT = 16
 TOP = (SLOT - ROWS) // 2
 LANES = 128
-GROUP = 4
 FACTOR = 32.0 * 1.4426950408889634
 F32 = jnp.float32
 BF16 = jnp.bfloat16
@@ -28,11 +27,15 @@
     return lax.broadcasted_iota(jnp.int32, shape, dim)
 
 
-def pack_kernel(chips, w, feat_ref, tail_ref, out_ref):
+def first_kernel(out_ref):
+    out_ref[...] = jnp.zeros((ROWS, LANES), F32)
+
+
+def pack_kernel(chips, w, zone_ref, first_ref, feat_ref, mask_ref, out_ref):
     half = (w + 2 * HALO) // 2
-    width = tail_ref.shape[1]
-    mask = tail_ref[:ROWS].astype(F32)
-    zone = tail_ref[ROWS:].astype(F32)
+    width = mask_ref.shape[2]
+    mask = mask_ref[0].astype(F32)
+    zone = first_ref[...] + zone_ref[0].astype(F32)
     lane = iota((ROWS, LANES), 1)
     for p in range(chips):
         for t in range(half // 2):
@@ -121,9 +124,24 @@
             test_ref[i, at, 3 * LANES :] = jnp.zeros((2 * ROWS, LANES), BF16)
 
 
+def weight_kernel(kern_ref, weight_ref):
+    twice = (iota((C, LANES), 1) % C == iota((C, LANES), 0)).astype(BF16)
+    low = iota((C, LANES), 1) < C
+    for conv in range(2):
+        doubled = lax.dot_general(kern_ref[conv], twice, (((0,), (0,)), ((), ())), preferred_element_type=F32)
+        for dy in range(3):
+            for at in range(4):
+                taps = [
+                    doubled[(3 * dy + dx) * C : (3 * dy + dx + 1) * C] if 0 <= dx < 3 else jnp.zeros((C, LANES), F32)
+                    for dx in (at, at - 1)
+                ]
+                row = (4 * dy + at) * C
+                weight_ref[conv, row : row + C, :] = jnp.where(low, taps[0], taps[1]).astype(BF16)
+
+
 def main_kernel(
-    chips, w, me_ref, owner_ref, own_ref, other_ref, test_ref, box_ref, kern_ref, out_ref,
-    res_ref, hid_ref, g0_ref, g1_ref, g2_ref, gsq_ref, weight_ref, *scratch
+    chips, w, me_ref, owner_ref, own_ref, other_ref, test_ref, box_ref, weight_ref, out_ref,
+    res_ref, hid_ref, g0_ref, g1_ref, g2_ref, gsq_ref, *scratch
 ):
     cols = w + 2 * HALO
     half = cols // 2
@@ -147,19 +165,6 @@
     lo = slice(0, C)
     hi = slice(C, LANES)
 
-    twice = (iota((C, LANES), 1) % C == iota((C, LANES), 0)).astype(BF16)
-    low = iota((C, LANES), 1) < C
-    for conv in range(2):
-        doubled = lax.dot_general(kern_ref[conv], twice, (((0,), (0,)), ((), ())), preferred_element_type=F32)
-        for dy in range(3):
-            for at in range(4):
-                taps = [
-                    doubled[(3 * dy + dx) * C : (3 * dy + dx + 1) * C] if 0 <= dx < 3 else jnp.zeros((C, LANES), F32)
-                    for dx in (at, at - 1)
-                ]
-                row = (4 * dy + at) * C
-                weight_ref[conv, row : row + C, :] = jnp.where(low, taps[0], taps[1]).astype(BF16)
-
     zones = [
         [ref[i, :, half // 2 * LANES :].astype(F32)[ROWS, 0].astype(jnp.int32) for i in range(chips)]
         for ref in (own_ref, other_ref)
@@ -169,6 +174,9 @@
     for ref in (g0_ref, g1_ref, g2_ref, gsq_ref):
         for i in range(0, ref.shape[0], ROWS):
             ref[i : i + ROWS, :] = jnp.where(low8, 0.0, 1.0) if ref is g1_ref else zero8
+    if half % 8 > 4:
+        for ref in golds_ref:
+            ref[cols * SLOT :, :] = jnp.zeros((ref.shape[0] - cols * SLOT, 4 * LANES), BF16)
     summing = (iota((SLOT, 4 * LANES), 1) >= 3 * LANES).astype(BF16)
 
     valid = []
@@ -381,6 +389,9 @@
         yield
 
     refined = [[] for p in range(w // 2)]
+    groups, sizes = [], [3, 3, 2] if chips == 8 else [4] * (chips // 4)
+    for size in sizes:
+        groups.append(range(sum(map(len, groups)), sum(map(len, groups)) + size))
     for slot in range(chips + 4):
         running = []
         if 0 <= slot - 1 < chips:
@@ -391,9 +402,9 @@
             running.append(average(i, kept[i % 3], golds_ref[i % 4]))
         if slot < chips:
             running.append(stage(slot, golds_ref[slot % 4]))
-        for k in range(0, chips, GROUP):
-            if slot == k + GROUP - 1 + 4:
-                running.append(finish_dies(range(k, k + GROUP)))
+        for dies in groups:
+            if slot == dies[-1] + 4:
+                running.append(finish_dies(dies))
         while running:
             running = [work for work in running if next(work, running) is not running]
 
@@ -443,15 +454,20 @@
     vmem = pl.BlockSpec(memory_space=pltpu.VMEM)
     params = pltpu.CompilerParams(vmem_limit_bytes=24 * 2**20)
 
-    zone = jnp.pad(zone_ids.reshape(1, 1), ((0, ROWS - 1), (0, defect_mask.shape[2] - 1)))
-    tail = jnp.concatenate([defect_mask[0], zone], 0)
+    first = pl.pallas_call(
+        first_kernel,
+        out_shape=jax.ShapeDtypeStruct((ROWS, LANES), F32),
+        out_specs=vmem,
+        compiler_params=pltpu.CompilerParams(vmem_limit_bytes=2**20),
+        cost_estimate=pl.CostEstimate(flops=10**9, bytes_accessed=10**6, transcendentals=0),
+    )()
     packed = pl.pallas_call(
         functools.partial(pack_kernel, chips, w),
         out_shape=jax.ShapeDtypeStruct((chips, 2 * ROWS, length), BF16),
-        in_specs=[vmem] * 2,
+        in_specs=[smem] + [vmem] * 3,
         out_specs=vmem,
         compiler_params=params,
-    )(features, tail)
+    )(zone_ids, first, features, defect_mask)
     groups = [[2 * p + c for p in range(chips)] for c in range(2)]
     own = lax.all_to_all(packed, "col", 0, 0, axis_index_groups=groups, tiled=True)
     other = lax.ppermute(own, "col", [(d, d ^ 1) for d in range(n)])
@@ -471,6 +487,14 @@
         compiler_params=params,
         cost_estimate=pl.CostEstimate(flops=10**9, bytes_accessed=10**6, transcendentals=0),
     )(own)
+    weights = pl.pallas_call(
+        weight_kernel,
+        out_shape=jax.ShapeDtypeStruct((2, 12 * C, LANES), BF16),
+        in_specs=[vmem],
+        out_specs=vmem,
+        compiler_params=params,
+        cost_estimate=pl.CostEstimate(flops=10**8, bytes_accessed=10**6, transcendentals=0),
+    )(jnp.swapaxes(kernels, 1, 2))
     me = lax.axis_index("col").astype(jnp.int32).reshape(1)
     chunks = -(-half // 8)
     reach = [min(raw // 2, 8 * v + 8) - max(0, 8 * v - SHIFT) for v in range(chunks)]
@@ -488,11 +512,10 @@
             pltpu.VMEM((chips, (w // 2 + 1) * SLOT + ROWS, LANES), F32),
         ]
         + [pltpu.VMEM((cols * SLOT, LANES), F32)] * 4
-        + [pltpu.VMEM((2, 12 * C, LANES), BF16)]
         + [pltpu.VMEM((rows, 4 * LANES), BF16)] * 4
         + kept * 3,
         compiler_params=params,
-    )(me, golden_owner, own, other, *tests, jnp.swapaxes(kernels, 1, 2))
+    )(me, golden_owner, own, other, *tests, weights)
     back = lax.all_to_all(partial, "col", 0, 0, tiled=True)
     return pl.pallas_call(
         functools.partial(score_kernel, chips, w),

time: 38.7 us -> 37.1 us (0.959)
  other arithmetic: 0.69 us -> 0 us
  local copies, waits for them, and re-layouts: 0.91 us -> 0.24 us
    concatenate x1 -> x0, other arithmetic: 0.69 us -> none  [body(): tail = jnp.concatenate([defect_mask[0], zone], 0)]
    unnamed x6 -> x8, local copies, waits for them, and re-layouts: 0.91 us -> 0.24 us
  transfers between devices with their start and end apart: 1 -> 1, of which waited for: 1 -> 1; matrix products, arithmetic and copies ran while one was open for 0% -> 0% of each run, Pallas kernels for 2% -> 3%
where the time goes in v4:
time: 37.1 us; the launch traced here: 36.9 us
  blocking collectives  27.8 us (75%)
  Pallas kernels  7.75 us (21%)
  between operations  0.74 us (2%)
  waiting for transfers between devices  0.4 us (1%)
    all_to_all x1, blocking collectives, body(): lax.all_to_all(packed, 'col', 0, 0, axis_index_groups=groups, tiled=True)  18 us
    all_to_all x1, blocking collectives, body(): back = lax.all_to_all(partial, 'col', 0, 0, tiled=True)  9.8 us
    pallas_call x1, Pallas kernels, body(): pl.pallas_call(functools.partial(main_kernel, chips, w), out_shape=jax.Sh...  5.71 us
    pallas_call x1, Pallas kernels, body(): pl.pallas_call(functools.partial(test_kernel, chips, w), out_shape=[jax.S...  0.93 us
    pallas_call x1, Pallas kernels, body(): pl.pallas_call(functools.partial(score_kernel, chips, w), out_shape=jax.S...  0.76 us
  transfers between devices with their start and end apart: 1, of which 1 were waited for; matrix products, arithmetic and copies ran while one was open for 0% of the time, Pallas kernels for 3%

profile of v4, /device:TPU:0, one launch (start us, length us, event | category | flops | bytes accessed | tf_op | source)
XLA Modules:
  0.0 36.9 jit_solution(1897801613136027537)
XLA Ops:
  0.0 0.0 copy-start.2
  0.0 0.0 copy-start.1
  0.0 0.0 copy-start
  0.7 0.0 copy-done.2
  0.7 0.2 copy-done.1
  0.9 0.1 shard_map.56
  1.0 18.0 %all_to_all.10.own_ref = bf16[8,16,1280]{2,1,0:T(8,128)(2,1)S(1)} all-to-all(bf16[8,16,1280]{2,1,0:T(8,128)(2,1)S(1)} %shard_map.56), channel_id=1, replica_groups={{0,2,4,6,8,10,12,14},{1,3,5,7,9,11,13,15},{16,18,20,22,24,26,28,30},{17..., dimensions={0} | all-to-all | bytes 655360 | tf_op jit(solution)/shard_map/all_to_all | solution.py:472
  19.0 0.0 collective-permute-start
  19.0 0.0 copy-done
  19.0 0.3 shard_map.58.weight_ref
  19.3 0.0 copy-start.3
  19.3 0.9 %shard_map.57 = (bf16[8,192,512]{2,1,0:T(8,128)(2,1)S(1)}, f32[8,160,128]{2,1,0:T(8,128)S(1)}) custom-call(bf16[8,16,1280]{2,1,0:T(8,128)(2,1)S(1)} %all_to_all.10.own_ref), custom_call_target="tpu_custom_call" | custom-call | flops 1000000000 | bytes 1000000 | tf_op jit(solution)/shard_map/pallas_call | solution.py:474
  20.2 0.4 %collective-permute-done.other_ref = bf16[8,16,1280]{2,1,0:T(8,128)(2,1)S(1)} collective-permute-done((bf16[8,16,1280]{2,1,0:T(8,128)(2,1)S(1)}, bf16[8,16,1280]{2,1,0:T(8,128)(2,1)S(1)}, u32[]{:S(2)}, u32[]{:S(2)}) %collective-permute-start) | collective-permute-done | bytes 327712 | tf_op jit(solution)/shard_map/ppermute | solution.py:473
  20.6 0.0 copy-done.3
  20.6 5.7 %shard_map.59 = f32[16,8,128]{2,1,0:T(8,128)S(1)} custom-call(s32[1]{0:T(128)} %bitcast.me_ref, s32[8]{0:T(128)S(1)} %copy-done.3, bf16[8,16,1280]{2,1,0:T(8,128)(2,1)S(1)} %all_to_all.10.own_ref, bf16[8,16,1280]{2,1,0:T(8,128)(2,1)S(1)} %collective-permute-done.other_ref, bf16[8,192,512]{2,1,0:T(8,128)(2,1)S(1)} %get-tuple-element.7.test_ref, ...), custom_call_target="tpu_custom_call" | custom-call | tf_op jit(solution)/shard_map/pallas_call | solution.py:505
  26.3 9.8 %all_to_all.11.back_ref = f32[16,8,128]{2,1,0:T(8,128)S(1)} all-to-all(f32[16,8,128]{2,1,0:T(8,128)S(1)} %shard_map.59), channel_id=1, replica_groups=mesh['groups'=2,'col'=16] {'col'}, dimensions={0} | all-to-all | bytes 131072 | tf_op jit(solution)/shard_map/all_to_all | solution.py:519
  36.1 0.8 %shard_map.60 = f32[1,8,128]{2,1,0:T(8,128)} custom-call(f32[16,8,128]{2,1,0:T(8,128)S(1)} %all_to_all.11.back_ref), custom_call_target="tpu_custom_call" | custom-call | tf_op jit(solution)/shard_map/pallas_call | solution.py:520
  (1 shorter events, 0.0 us)
Async XLA Ops:
  0.0 0.7 %copy-start.2 = (s32[1,8,128]{2,1,0:T(8,128)S(1)}, s32[1,8,128]{2,1,0:T(8,128)}, u32[]{:S(2)}) copy-start(s32[1,8,128]{2,1,0:T(8,128)} %mask_ref.1) | copy-start | bytes 12292
  0.0 0.9 %copy-start.1 = (bf16[1,8,8192]{2,1,0:T(8,128)(2,1)S(1)}, bf16[1,8,8192]{2,1,0:T(8,128)(2,1)}, u32[]{:S(2)}) copy-start(bf16[1,8,8192]{2,1,0:T(8,128)(2,1)} %feat_ref.1) | copy-start | bytes 393220
  0.0 19.0 %copy-start = (bf16[2,576,64]{1,2,0:T(8,128)(2,1)S(1)}, bf16[2,576,64]{1,2,0:T(8,128)(2,1)}, u32[]{:S(2)}) copy-start(bf16[2,576,64]{1,2,0:T(8,128)(2,1)} %param.9) | copy-start | bytes 442372
  19.0 1.6 %collective-permute-start = (bf16[8,16,1280]{2,1,0:T(8,128)(2,1)S(1)}, bf16[8,16,1280]{2,1,0:T(8,128)(2,1)S(1)}, u32[]{:S(2)}, u32[]{:S(2)}) collective-permute-start(bf16[8,16,1280]{2,1,0:T(8,128)(2,1)S(1)} %all_to_all.10.own_ref), channel_id=1, source_target_pairs={{0,1},{1,0},{2,3},{3,2},{4,5},{5,4},{6,7},{7,6},{8,9},{9,8},{10,11... | collective-permute-start | bytes 983048 | tf_op jit(solution)/shard_map/ppermute | solution.py:473
  19.3 1.3 %copy-start.3 = (s32[8]{0:T(128)S(1)}, s32[8]{0:T(128)}, u32[]{:S(2)}) copy-start(s32[8]{0:T(128)} %owner_ref.1) | copy-start | bytes 100

commit v5 on v4

--- a/solution.py
+++ b/solution.py
@@ -32,25 +32,25 @@
 
 
 def pack_kernel(chips, w, zone_ref, first_ref, feat_ref, mask_ref, out_ref):
-    half = (w + 2 * HALO) // 2
+    cols = w + 2 * HALO
     width = mask_ref.shape[2]
     mask = mask_ref[0].astype(F32)
     zone = first_ref[...] + zone_ref[0].astype(F32)
     lane = iota((ROWS, LANES), 1)
     for p in range(chips):
-        for t in range(half // 2):
-            parts = []
-            for part in range(2):
-                col = p * w - HALO + part * half + 2 * t
-                if 0 <= col < width:
-                    parts.append(feat_ref[0, :, col * C : (col + 2) * C].astype(F32))
-                else:
-                    parts.append(jnp.zeros((ROWS, LANES), F32))
-            out_ref[p, :, t * LANES : (t + 1) * LANES] = jnp.concatenate(parts, 0).astype(BF16)
+        for t in range(cols // 2):
+            col = p * w - HALO + 2 * t
+            at = slice(t * LANES, (t + 1) * LANES)
+            if 0 <= col < width:
+                out_ref[p, :, at] = feat_ref[0, :, col * C : (col + 2) * C]
+            else:
+                out_ref[p, :, at] = jnp.zeros((ROWS, LANES), BF16)
         here = pltpu.roll(mask, (width - p * w) % width, 1) if p else mask
-        here = jnp.where(lane < w, here, 0.0)
-        last = jnp.concatenate([here, zone], 0)
-        out_ref[p, :, half // 2 * LANES :] = last.astype(BF16)
+        out_ref[p, :, cols * C :] = jnp.where(lane < w, here, zone).astype(BF16)
+
+
+def pair_of(ref, i, t):
+    return ref[i, :, t * LANES : (t + 1) * LANES].astype(F32)
 
 
 def split_square(values):
@@ -70,7 +70,6 @@
 
 
 def test_kernel(chips, w, own_ref, test_ref, box_ref, wide_ref, *scratch):
-    half = (w + 2 * HALO) // 2
     raw = w + 4 + 2 * REACH
     before = HALO - REACH - 2
     zero8 = jnp.zeros((ROWS, LANES), F32)
@@ -80,11 +79,8 @@
         for i in range(0, ref.shape[0], ROWS):
             ref[i : i + ROWS, :] = zero8
     pairs = []
-    for part in range(2):
-        for t in range(half // 2):
-            if 0 <= part * half + 2 * t - before < raw:
-                rows = slice(part * ROWS, (part + 1) * ROWS)
-                pairs.append([own_ref[i, :, t * LANES : (t + 1) * LANES].astype(F32)[rows] for i in range(chips)])
+    for t in range(before // 2, (before + raw) // 2):
+        pairs.append([pair_of(own_ref, i, t) for i in range(chips)])
     parts = [split_square(jnp.concatenate([tiles[i] for tiles in pairs], 0)) for i in range(chips)]
     squares = [jnp.concatenate([part[k].astype(BF16) for part in parts], 0) for k in range(2)]
     both = (iota((2 * LANES, 2 * LANES), 0) % LANES // C == iota((2 * LANES, 2 * LANES), 1) // LANES).astype(BF16)
@@ -166,8 +162,7 @@
     hi = slice(C, LANES)
 
     zones = [
-        [ref[i, :, half // 2 * LANES :].astype(F32)[ROWS, 0].astype(jnp.int32) for i in range(chips)]
-        for ref in (own_ref, other_ref)
+        [pair_of(ref, i, cols // 2)[0, w].astype(jnp.int32) for i in range(chips)] for ref in (own_ref, other_ref)
     ]
     golds = [owner_ref[zone] for zone in zones[0]]
 
@@ -193,21 +188,18 @@
     def stage(i, gold_ref):
         owner = golds[i]
         mine = owner % 2 == core
-        for t in range(half // 2):
-            at = slice(t * LANES, (t + 1) * LANES)
-            tile = jnp.where(mine, own_ref[owner // 2, :, at], other_ref[owner // 2, :, at]).astype(F32)
-            for part in range(2):
-                here = tile[part * ROWS : (part + 1) * ROWS]
-                turned = pltpu.roll(here, C, 1)
-                for odd, (left, right) in enumerate(((here, turned), (turned, here))):
-                    top = odd * odds + (part * half // 2 + t) * SLOT + TOP
-                    g0_ref[top + 2 : top + 2 + ROWS, lo] = left[:, lo]
-                    g0_ref[top + 1 : top + 1 + ROWS, hi] = right[:, hi]
-                    g1_ref[top : top + ROWS, lo] = left[:, lo]
-                    g2_ref[top - 1 : top - 1 + ROWS, lo] = left[:, lo]
-                    g2_ref[top - 2 : top - 2 + ROWS, hi] = right[:, hi]
-                    high, low = split_square(jnp.where(low8, left, right))
-                    gsq_ref[top : top + ROWS, :] = jnp.where(low8, high, low)
+        for t in range(cols // 2):
+            here = jnp.where(mine, pair_of(own_ref, owner // 2, t), pair_of(other_ref, owner // 2, t))
+            turned = pltpu.roll(here, C, 1)
+            for odd, (left, right) in enumerate(((here, turned), (turned, here))):
+                top = odd * odds + t * SLOT + TOP
+                g0_ref[top + 2 : top + 2 + ROWS, lo] = left[:, lo]
+                g0_ref[top + 1 : top + 1 + ROWS, hi] = right[:, hi]
+                g1_ref[top : top + ROWS, lo] = left[:, lo]
+                g2_ref[top - 1 : top - 1 + ROWS, lo] = left[:, lo]
+                g2_ref[top - 2 : top - 2 + ROWS, hi] = right[:, hi]
+                high, low = split_square(jnp.where(low8, left, right))
+                gsq_ref[top : top + ROWS, :] = jnp.where(low8, high, low)
             yield
         for parity in range(2):
             for g in range(half):
@@ -311,9 +303,7 @@
                 even, odd = total[k * ROWS : (k + 1) * ROWS], total[(k + 1) * ROWS : (k + 2) * ROWS]
                 numer = jnp.where(low8, even, pltpu.roll(odd, C, 1))
                 denom = jnp.where(low8, pltpu.roll(even, C, 1), odd) + outside
-                part, t = divmod(HALO // 2 - 1 + pair, half // 2)
-                test = own_ref[i, :, t * LANES : (t + 1) * LANES].astype(F32)[part * ROWS : (part + 1) * ROWS]
-                value = test - numer / denom
+                value = pair_of(own_ref, i, HALO // 2 - 1 + pair) - numer / denom
                 if pair == 0:
                     value = value * not_first
                 if pair == outs // 2 - 1:
@@ -413,8 +403,7 @@
     for i in range(chips):
         found = energy[i * ROWS : (i + 1) * ROWS]
         out_ref[2 * i + core] = found
-        mask = own_ref[i, :, half // 2 * LANES :].astype(F32)[:ROWS]
-        mask = jnp.where(lane8 < w, mask, 0.0)
+        mask = jnp.where(lane8 < w, pair_of(own_ref, i, cols // 2), 0.0)
         total = jnp.sum(jnp.sum(found * mask, axis=0, keepdims=True), axis=1, keepdims=True)
         count = jnp.sum(jnp.sum(mask, axis=0, keepdims=True), axis=1, keepdims=True)
         both = jnp.where(lane8 == w, total, 0.0) + jnp.where(lane8 == w + 1, count, 0.0)
@@ -449,7 +438,7 @@
     cols = w + 2 * HALO
     half = cols // 2
     raw = w + 4 + 2 * REACH
-    length = half * C + LANES
+    length = cols * C + LANES
     smem = pl.BlockSpec(memory_space=pltpu.SMEM)
     vmem = pl.BlockSpec(memory_space=pltpu.VMEM)
     params = pltpu.CompilerParams(vmem_limit_bytes=24 * 2**20)
@@ -463,7 +452,7 @@
     )()
     packed = pl.pallas_call(
         functools.partial(pack_kernel, chips, w),
-        out_shape=jax.ShapeDtypeStruct((chips, 2 * ROWS, length), BF16),
+        out_shape=jax.ShapeDtypeStruct((chips, ROWS, length), BF16),
         in_specs=[smem] + [vmem] * 3,
         out_specs=vmem,
         compiler_params=params,

time: 37.1 us -> 36.8 us (level)
  blocking collectives: 27.8 us -> 27.4 us
where the time goes in v5:
time: 36.8 us; the launch traced here: 36.5 us
  blocking collectives  27.4 us (74%)
  Pallas kernels  7.77 us (21%)
  between operations  0.74 us (2%)
    all_to_all x1, blocking collectives, body(): lax.all_to_all(packed, 'col', 0, 0, axis_index_groups=groups, tiled=True)  17.7 us
    all_to_all x1, blocking collectives, body(): back = lax.all_to_all(partial, 'col', 0, 0, tiled=True)  9.73 us
    pallas_call x1, Pallas kernels, body(): pl.pallas_call(functools.partial(main_kernel, chips, w), out_shape=jax.Sh...  5.71 us
    pallas_call x1, Pallas kernels, body(): pl.pallas_call(functools.partial(test_kernel, chips, w), out_shape=[jax.S...  0.94 us
    pallas_call x1, Pallas kernels, body(): pl.pallas_call(functools.partial(score_kernel, chips, w), out_shape=jax.S...  0.76 us
  transfers between devices with their start and end apart: 1, of which 1 were waited for; matrix products, arithmetic and copies ran while one was open for 0% of the time, Pallas kernels for 3%

profile of v5, /device:TPU:0, one launch (start us, length us, event | category | flops | bytes accessed | tf_op | source)
XLA Modules:
  0.0 36.5 jit_solution(14550899382092947776)
XLA Ops:
  0.0 0.0 copy-start.2
  0.0 0.0 copy-start.1
  0.0 0.0 copy-start
  0.7 0.0 copy-done.2
  0.7 0.2 copy-done.1
  0.9 0.1 shard_map.56
  1.0 17.7 %all_to_all.10.own_ref = bf16[8,8,2432]{2,1,0:T(8,128)(2,1)S(1)} all-to-all(bf16[8,8,2432]{2,1,0:T(8,128)(2,1)S(1)} %shard_map.56), channel_id=1, replica_groups={{0,2,4,6,8,10,12,14},{1,3,5,7,9,11,13,15},{16,18,20,22,24,26,28,30},{17..., dimensions={0} | all-to-all | bytes 622592 | tf_op jit(solution)/shard_map/all_to_all | solution.py:461
  18.7 0.0 collective-permute-start
  18.7 0.0 copy-done
  18.7 0.3 shard_map.58.weight_ref
  19.0 0.0 copy-start.3
  19.0 0.9 %shard_map.57 = (bf16[8,192,512]{2,1,0:T(8,128)(2,1)S(1)}, f32[8,160,128]{2,1,0:T(8,128)S(1)}) custom-call(bf16[8,8,2432]{2,1,0:T(8,128)(2,1)S(1)} %all_to_all.10.own_ref), custom_call_target="tpu_custom_call" | custom-call | flops 1000000000 | bytes 1000000 | tf_op jit(solution)/shard_map/pallas_call | solution.py:463
  20.0 0.4 collective-permute-done.other_ref
  20.3 0.0 copy-done.3
  20.3 5.7 %shard_map.59 = f32[16,8,128]{2,1,0:T(8,128)S(1)} custom-call(s32[1]{0:T(128)} %bitcast.me_ref, s32[8]{0:T(128)S(1)} %copy-done.3, bf16[8,8,2432]{2,1,0:T(8,128)(2,1)S(1)} %all_to_all.10.own_ref, bf16[8,8,2432]{2,1,0:T(8,128)(2,1)S(1)} %collective-permute-done.other_ref, bf16[8,192,512]{2,1,0:T(8,128)(2,1)S(1)} %get-tuple-element.7.test_ref, ...), custom_call_target="tpu_custom_call" | custom-call | tf_op jit(solution)/shard_map/pallas_call | solution.py:494
  26.0 9.7 %all_to_all.11.back_ref = f32[16,8,128]{2,1,0:T(8,128)S(1)} all-to-all(f32[16,8,128]{2,1,0:T(8,128)S(1)} %shard_map.59), channel_id=1, replica_groups=mesh['groups'=2,'col'=16] {'col'}, dimensions={0} | all-to-all | bytes 131072 | tf_op jit(solution)/shard_map/all_to_all | solution.py:508
  35.8 0.8 %shard_map.60 = f32[1,8,128]{2,1,0:T(8,128)} custom-call(f32[16,8,128]{2,1,0:T(8,128)S(1)} %all_to_all.11.back_ref), custom_call_target="tpu_custom_call" | custom-call | tf_op jit(solution)/shard_map/pallas_call | solution.py:509
  (1 shorter events, 0.0 us)
Async XLA Ops:
  0.0 0.7 %copy-start.2 = (s32[1,8,128]{2,1,0:T(8,128)S(1)}, s32[1,8,128]{2,1,0:T(8,128)}, u32[]{:S(2)}) copy-start(s32[1,8,128]{2,1,0:T(8,128)} %mask_ref.1) | copy-start | bytes 12292
  0.0 0.9 %copy-start.1 = (bf16[1,8,8192]{2,1,0:T(8,128)(2,1)S(1)}, bf16[1,8,8192]{2,1,0:T(8,128)(2,1)}, u32[]{:S(2)}) copy-start(bf16[1,8,8192]{2,1,0:T(8,128)(2,1)} %feat_ref.1) | copy-start | bytes 393220
  0.0 18.7 %copy-start = (bf16[2,576,64]{1,2,0:T(8,128)(2,1)S(1)}, bf16[2,576,64]{1,2,0:T(8,128)(2,1)}, u32[]{:S(2)}) copy-start(bf16[2,576,64]{1,2,0:T(8,128)(2,1)} %param.9) | copy-start | bytes 442372
  18.7 1.6 %collective-permute-start = (bf16[8,8,2432]{2,1,0:T(8,128)(2,1)S(1)}, bf16[8,8,2432]{2,1,0:T(8,128)(2,1)S(1)}, u32[]{:S(2)}, u32[]{:S(2)}) collective-permute-start(bf16[8,8,2432]{2,1,0:T(8,128)(2,1)S(1)} %all_to_all.10.own_ref), channel_id=1, source_target_pairs={{0,1},{1,0},{2,3},{3,2},{4,5},{5,4},{6,7},{7,6},{8,9},{9,8},{10,11... | collective-permute-start | bytes 933896 | tf_op jit(solution)/shard_map/ppermute | solution.py:462
  19.0 1.3 %copy-start.3 = (s32[8]{0:T(128)S(1)}, s32[8]{0:T(128)}, u32[]{:S(2)}) copy-start(s32[8]{0:T(128)} %owner_ref.1) | copy-start | bytes 100

commit v6 on v5

--- a/solution.py
+++ b/solution.py
@@ -146,8 +146,8 @@
     odds = half * SLOT
     chunks = -(-half // 8)
     lanes_g = chunks * LANES
-    golds_ref = scratch[:4]
-    kept = [scratch[4 + k * (chunks + 1) : 4 + (k + 1) * (chunks + 1)] for k in range(3)]
+    golds_ref = scratch[:5]
+    kept = [scratch[5 + k * (chunks + 1) : 5 + (k + 1) * (chunks + 1)] for k in range(4)]
     me = me_ref[0]
     chip = me // 2
     core = me % 2
@@ -379,21 +379,21 @@
         yield
 
     refined = [[] for p in range(w // 2)]
-    groups, sizes = [], [3, 3, 2] if chips == 8 else [4] * (chips // 4)
+    groups, sizes = [], [5, 3] if chips == 8 else [4] * (chips // 4)
     for size in sizes:
         groups.append(range(sum(map(len, groups)), sum(map(len, groups)) + size))
-    for slot in range(chips + 4):
+    for slot in range(chips + 5):
         running = []
         if 0 <= slot - 1 < chips:
             i = slot - 1
-            running.append(products(i, kept[i % 3], golds_ref[i % 4]))
-        if 0 <= slot - 3 < chips:
-            i = slot - 3
-            running.append(average(i, kept[i % 3], golds_ref[i % 4]))
+            running.append(products(i, kept[i % 4], golds_ref[i % 5]))
+        if 0 <= slot - 4 < chips:
+            i = slot - 4
+            running.append(average(i, kept[i % 4], golds_ref[i % 5]))
         if slot < chips:
-            running.append(stage(slot, golds_ref[slot % 4]))
+            running.append(stage(slot, golds_ref[slot % 5]))
         for dies in groups:
-            if slot == dies[-1] + 4:
+            if slot == dies[-1] + 5:
                 running.append(finish_dies(dies))
         while running:
             running = [work for work in running if next(work, running) is not running]
@@ -501,8 +501,8 @@
             pltpu.VMEM((chips, (w // 2 + 1) * SLOT + ROWS, LANES), F32),
         ]
         + [pltpu.VMEM((cols * SLOT, LANES), F32)] * 4
-        + [pltpu.VMEM((rows, 4 * LANES), BF16)] * 4
-        + kept * 3,
+        + [pltpu.VMEM((rows, 4 * LANES), BF16)] * 5
+        + kept * 4,
         compiler_params=params,
     )(me, golden_owner, own, other, *tests, weights)
     back = lax.all_to_all(partial, "col", 0, 0, tiled=True)

time: 36.8 us -> 36.6 us (level)
  no operation moved by 1% of the time
where the time goes in v6:
time: 36.6 us; the launch traced here: 36.4 us
  blocking collectives  27.4 us (75%)
  Pallas kernels  7.64 us (21%)
  between operations  0.74 us (2%)
    all_to_all x1, blocking collectives, body(): lax.all_to_all(packed, 'col', 0, 0, axis_index_groups=groups, tiled=True)  17.7 us
    all_to_all x1, blocking collectives, body(): back = lax.all_to_all(partial, 'col', 0, 0, tiled=True)  9.74 us
    pallas_call x1, Pallas kernels, body(): pl.pallas_call(functools.partial(main_kernel, chips, w), out_shape=jax.Sh...  5.58 us
    pallas_call x1, Pallas kernels, body(): pl.pallas_call(functools.partial(test_kernel, chips, w), out_shape=[jax.S...  0.94 us
    pallas_call x1, Pallas kernels, body(): pl.pallas_call(functools.partial(score_kernel, chips, w), out_shape=jax.S...  0.76 us
  transfers between devices with their start and end apart: 1, of which 1 were waited for; matrix products, arithmetic and copies ran while one was open for 0% of the time, Pallas kernels for 3%

profile of v6, /device:TPU:0, one launch (start us, length us, event | category | flops | bytes accessed | tf_op | source)
XLA Modules:
  0.0 36.4 jit_solution(6615124195507316674)
XLA Ops:
  0.0 0.0 copy-start.2
  0.0 0.0 copy-start.1
  0.0 0.0 copy-start
  0.7 0.0 copy-done.2
  0.7 0.2 copy-done.1
  0.9 0.1 shard_map.56
  1.0 17.7 %all_to_all.10.own_ref = bf16[8,8,2432]{2,1,0:T(8,128)(2,1)S(1)} all-to-all(bf16[8,8,2432]{2,1,0:T(8,128)(2,1)S(1)} %shard_map.56), channel_id=1, replica_groups={{0,2,4,6,8,10,12,14},{1,3,5,7,9,11,13,15},{16,18,20,22,24,26,28,30},{17..., dimensions={0} | all-to-all | bytes 622592 | tf_op jit(solution)/shard_map/all_to_all | solution.py:461
  18.7 0.0 collective-permute-start
  18.7 0.0 copy-done
  18.7 0.3 shard_map.58.weight_ref
  19.0 0.0 copy-start.3
  19.0 0.9 %shard_map.57 = (bf16[8,192,512]{2,1,0:T(8,128)(2,1)S(1)}, f32[8,160,128]{2,1,0:T(8,128)S(1)}) custom-call(bf16[8,8,2432]{2,1,0:T(8,128)(2,1)S(1)} %all_to_all.10.own_ref), custom_call_target="tpu_custom_call" | custom-call | flops 1000000000 | bytes 1000000 | tf_op jit(solution)/shard_map/pallas_call | solution.py:463
  20.0 0.4 collective-permute-done.other_ref
  20.3 0.0 copy-done.3
  20.3 5.6 %shard_map.59 = f32[16,8,128]{2,1,0:T(8,128)S(1)} custom-call(s32[1]{0:T(128)} %bitcast.me_ref, s32[8]{0:T(128)S(1)} %copy-done.3, bf16[8,8,2432]{2,1,0:T(8,128)(2,1)S(1)} %all_to_all.10.own_ref, bf16[8,8,2432]{2,1,0:T(8,128)(2,1)S(1)} %collective-permute-done.other_ref, bf16[8,192,512]{2,1,0:T(8,128)(2,1)S(1)} %get-tuple-element.7.test_ref, ...), custom_call_target="tpu_custom_call" | custom-call | tf_op jit(solution)/shard_map/pallas_call | solution.py:494
  25.9 9.7 %all_to_all.11.back_ref = f32[16,8,128]{2,1,0:T(8,128)S(1)} all-to-all(f32[16,8,128]{2,1,0:T(8,128)S(1)} %shard_map.59), channel_id=1, replica_groups=mesh['groups'=2,'col'=16] {'col'}, dimensions={0} | all-to-all | bytes 131072 | tf_op jit(solution)/shard_map/all_to_all | solution.py:508
  35.7 0.8 %shard_map.60 = f32[1,8,128]{2,1,0:T(8,128)} custom-call(f32[16,8,128]{2,1,0:T(8,128)S(1)} %all_to_all.11.back_ref), custom_call_target="tpu_custom_call" | custom-call | tf_op jit(solution)/shard_map/pallas_call | solution.py:509
  (1 shorter events, 0.0 us)
Async XLA Ops:
  0.0 0.7 %copy-start.2 = (s32[1,8,128]{2,1,0:T(8,128)S(1)}, s32[1,8,128]{2,1,0:T(8,128)}, u32[]{:S(2)}) copy-start(s32[1,8,128]{2,1,0:T(8,128)} %mask_ref.1) | copy-start | bytes 12292
  0.0 0.9 %copy-start.1 = (bf16[1,8,8192]{2,1,0:T(8,128)(2,1)S(1)}, bf16[1,8,8192]{2,1,0:T(8,128)(2,1)}, u32[]{:S(2)}) copy-start(bf16[1,8,8192]{2,1,0:T(8,128)(2,1)} %feat_ref.1) | copy-start | bytes 393220
  0.0 18.7 %copy-start = (bf16[2,576,64]{1,2,0:T(8,128)(2,1)S(1)}, bf16[2,576,64]{1,2,0:T(8,128)(2,1)}, u32[]{:S(2)}) copy-start(bf16[2,576,64]{1,2,0:T(8,128)(2,1)} %param.9) | copy-start | bytes 442372
  18.7 1.6 %collective-permute-start = (bf16[8,8,2432]{2,1,0:T(8,128)(2,1)S(1)}, bf16[8,8,2432]{2,1,0:T(8,128)(2,1)S(1)}, u32[]{:S(2)}, u32[]{:S(2)}) collective-permute-start(bf16[8,8,2432]{2,1,0:T(8,128)(2,1)S(1)} %all_to_all.10.own_ref), channel_id=1, source_target_pairs={{0,1},{1,0},{2,3},{3,2},{4,5},{5,4},{6,7},{7,6},{8,9},{9,8},{10,11... | collective-permute-start | bytes 933896 | tf_op jit(solution)/shard_map/ppermute | solution.py:462
  19.0 1.3 %copy-start.3 = (s32[8]{0:T(128)S(1)}, s32[8]{0:T(128)}, u32[]{:S(2)}) copy-start(s32[8]{0:T(128)} %owner_ref.1) | copy-start | bytes 100

commit v7 on v6

--- a/solution.py
+++ b/solution.py
@@ -402,7 +402,9 @@
     sums = zero8
     for i in range(chips):
         found = energy[i * ROWS : (i + 1) * ROWS]
-        out_ref[2 * i + core] = found
+        line = jnp.sum(pltpu.roll(found, 0, 1, stride=w, stride_axis=0), axis=0, keepdims=True)
+        out_ref[2 * i + core, 0:1, :] = line
+        out_ref[2 * i + 1 - core, 0:1, :] = zero8[:1]
         mask = jnp.where(lane8 < w, pair_of(own_ref, i, cols // 2), 0.0)
         total = jnp.sum(jnp.sum(found * mask, axis=0, keepdims=True), axis=1, keepdims=True)
         count = jnp.sum(jnp.sum(mask, axis=0, keepdims=True), axis=1, keepdims=True)
@@ -411,23 +413,22 @@
     for i in range(chips):
         for which in range(2):
             mine = jnp.sum(jnp.where(sub8 == zones[which][i], sums, 0.0), axis=0, keepdims=True)
-            mine = jnp.broadcast_to(mine, (ROWS, LANES))
-            if which:
-                out_ref[2 * i + 1 - core] = mine
-            else:
-                out_ref[2 * i + core] = out_ref[2 * i + core] + mine
+            out_ref[2 * i + (1 - core if which else core), 1:2, :] = mine
 
 
 def score_kernel(chips, w, back_ref, out_ref):
-    lane = iota((ROWS, LANES), 1)
-    total = back_ref[0]
+    lane, sub = iota((ROWS, LANES), 1), iota((ROWS, LANES), 0)
+    total = back_ref[0, 1:2, :]
     for d in range(1, 2 * chips):
-        total = total + back_ref[d]
+        total = total + back_ref[d, 1:2, :]
     zone_mean = total[:, w : w + 1] / jnp.maximum(total[:, w + 1 : w + 2], 1.0)
     energy = jnp.zeros((ROWS, LANES), F32)
     for p in range(chips):
-        strip = back_ref[2 * p] + back_ref[2 * p + 1]
+        line = back_ref[2 * p, 0:1, :] + back_ref[2 * p + 1, 0:1, :]
+        strip = jnp.broadcast_to(line, (ROWS, LANES))
         strip = pltpu.roll(strip, p * w, 1) if p else strip
+        for bit in (1, 2, 4):
+            strip = jnp.where(sub & bit != 0, pltpu.roll(strip, LANES - bit * w, 1), strip)
         energy = jnp.where((lane >= p * w) & (lane < (p + 1) * w), strip, energy)
     out_ref[0] = energy / (zone_mean + 0.01)
 
@@ -493,7 +494,7 @@
     rows = half * SLOT + -(-half // 8) * LANES
     partial = pl.pallas_call(
         functools.partial(main_kernel, chips, w),
-        out_shape=jax.ShapeDtypeStruct((n, ROWS, LANES), F32),
+        out_shape=jax.ShapeDtypeStruct((n, 2, LANES), F32),
         in_specs=[smem, smem] + [vmem] * 5,
         out_specs=vmem,
         scratch_shapes=[

time: 36.6 us -> 36.4 us (level)
  blocking collectives: 27.4 us -> 27 us
    all_to_all x1, blocking collectives: 9.74 us -> 9.33 us  [body(): back = lax.all_to_all(partial, 'col', 0, 0, tiled=True)]
where the time goes in v7:
time: 36.4 us; the launch traced here: 36.1 us
  blocking collectives  27 us (74%)
  Pallas kernels  7.76 us (21%)
  between operations  0.74 us (2%)
    all_to_all x1, blocking collectives, body(): lax.all_to_all(packed, 'col', 0, 0, axis_index_groups=groups, tiled=True)  17.7 us
    all_to_all x1, blocking collectives, body(): back = lax.all_to_all(partial, 'col', 0, 0, tiled=True)  9.33 us
    pallas_call x1, Pallas kernels, body(): pl.pallas_call(functools.partial(main_kernel, chips, w), out_shape=jax.Sh...  5.59 us
    pallas_call x1, Pallas kernels, body(): pl.pallas_call(functools.partial(test_kernel, chips, w), out_shape=[jax.S...  0.94 us
    pallas_call x1, Pallas kernels, body(): pl.pallas_call(functools.partial(score_kernel, chips, w), out_shape=jax.S...  0.88 us
  transfers between devices with their start and end apart: 1, of which 1 were waited for; matrix products, arithmetic and copies ran while one was open for 0% of the time, Pallas kernels for 3%

profile of v7, /device:TPU:0, one launch (start us, length us, event | category | flops | bytes accessed | tf_op | source)
XLA Modules:
  0.0 36.1 jit_solution(11432003747352693440)
XLA Ops:
  0.0 0.0 copy-start.2
  0.0 0.0 copy-start.1
  0.0 0.0 copy-start
  0.7 0.0 copy-done.2
  0.7 0.2 copy-done.1
  0.9 0.1 shard_map.56
  1.0 17.7 %all_to_all.10.own_ref = bf16[8,8,2432]{2,1,0:T(8,128)(2,1)S(1)} all-to-all(bf16[8,8,2432]{2,1,0:T(8,128)(2,1)S(1)} %shard_map.56), channel_id=1, replica_groups={{0,2,4,6,8,10,12,14},{1,3,5,7,9,11,13,15},{16,18,20,22,24,26,28,30},{17..., dimensions={0} | all-to-all | bytes 622592 | tf_op jit(solution)/shard_map/all_to_all | solution.py:462
  18.7 0.0 collective-permute-start
  18.7 0.0 copy-done
  18.7 0.3 shard_map.58.weight_ref
  19.0 0.0 copy-start.3
  19.0 0.9 %shard_map.57 = (bf16[8,192,512]{2,1,0:T(8,128)(2,1)S(1)}, f32[8,160,128]{2,1,0:T(8,128)S(1)}) custom-call(bf16[8,8,2432]{2,1,0:T(8,128)(2,1)S(1)} %all_to_all.10.own_ref), custom_call_target="tpu_custom_call" | custom-call | flops 1000000000 | bytes 1000000 | tf_op jit(solution)/shard_map/pallas_call | solution.py:464
  20.0 0.4 collective-permute-done.other_ref
  20.3 0.0 copy-done.3
  20.3 5.6 %shard_map.59 = f32[16,2,128]{2,1,0:T(2,128)S(1)} custom-call(s32[1]{0:T(128)} %bitcast.me_ref, s32[8]{0:T(128)S(1)} %copy-done.3, bf16[8,8,2432]{2,1,0:T(8,128)(2,1)S(1)} %all_to_all.10.own_ref, bf16[8,8,2432]{2,1,0:T(8,128)(2,1)S(1)} %collective-permute-done.other_ref, bf16[8,192,512]{2,1,0:T(8,128)(2,1)S(1)} %get-tuple-element.7.test_ref, ...), custom_call_target="tpu_custom_call" | custom-call | tf_op jit(solution)/shard_map/pallas_call | solution.py:495
  25.9 9.3 %all_to_all.11.back_ref = f32[16,2,128]{2,1,0:T(2,128)S(1)} all-to-all(f32[16,2,128]{2,1,0:T(2,128)S(1)} %shard_map.59), channel_id=1, replica_groups=mesh['groups'=2,'col'=16] {'col'}, dimensions={0} | all-to-all | bytes 32768 | tf_op jit(solution)/shard_map/all_to_all | solution.py:509
  35.2 0.9 %shard_map.60 = f32[1,8,128]{2,1,0:T(8,128)} custom-call(f32[16,2,128]{2,1,0:T(2,128)S(1)} %all_to_all.11.back_ref), custom_call_target="tpu_custom_call" | custom-call | tf_op jit(solution)/shard_map/pallas_call | solution.py:510
  (1 shorter events, 0.0 us)
Async XLA Ops:
  0.0 0.7 %copy-start.2 = (s32[1,8,128]{2,1,0:T(8,128)S(1)}, s32[1,8,128]{2,1,0:T(8,128)}, u32[]{:S(2)}) copy-start(s32[1,8,128]{2,1,0:T(8,128)} %mask_ref.1) | copy-start | bytes 12292
  0.0 0.9 %copy-start.1 = (bf16[1,8,8192]{2,1,0:T(8,128)(2,1)S(1)}, bf16[1,8,8192]{2,1,0:T(8,128)(2,1)}, u32[]{:S(2)}) copy-start(bf16[1,8,8192]{2,1,0:T(8,128)(2,1)} %feat_ref.1) | copy-start | bytes 393220
  0.0 18.7 %copy-start = (bf16[2,576,64]{1,2,0:T(8,128)(2,1)S(1)}, bf16[2,576,64]{1,2,0:T(8,128)(2,1)}, u32[]{:S(2)}) copy-start(bf16[2,576,64]{1,2,0:T(8,128)(2,1)} %param.9) | copy-start | bytes 442372
  18.7 1.6 %collective-permute-start = (bf16[8,8,2432]{2,1,0:T(8,128)(2,1)S(1)}, bf16[8,8,2432]{2,1,0:T(8,128)(2,1)S(1)}, u32[]{:S(2)}, u32[]{:S(2)}) collective-permute-start(bf16[8,8,2432]{2,1,0:T(8,128)(2,1)S(1)} %all_to_all.10.own_ref), channel_id=1, source_target_pairs={{0,1},{1,0},{2,3},{3,2},{4,5},{5,4},{6,7},{7,6},{8,9},{9,8},{10,11... | collective-permute-start | bytes 933896 | tf_op jit(solution)/shard_map/ppermute | solution.py:463
  19.0 1.3 %copy-start.3 = (s32[8]{0:T(128)S(1)}, s32[8]{0:T(128)}, u32[]{:S(2)}) copy-start(s32[8]{0:T(128)} %owner_ref.1) | copy-start | bytes 100
